TPU v7x, 256 devices: a whole 4x4x8 slice. The times are simulated.
256 devices in a mesh: gx: 8 (over y_lo, x), gy: 8 (over z), gz: 4 (over y_hi, core).
Axes of the slice: x: 4, y: 4 (y_hi: 2, y_lo: 2; y = y_hi * 2 + y_lo), z: 8, core: 2. Of those that a mesh axis runs over, the one named last changes fastest.
Arguments:
- cells: int32 [524288], P(('gx', 'gy', 'gz')), may hold values from 0 to 63
- offsets: float32 [3, 524288], P(None, ('gx', 'gy', 'gz')), may hold values from 0.5 to 1.5
- velocity: float32 [3, 524288], P(None, ('gx', 'gy', 'gz')), may hold values from -6 to 6
- affine: float32 [9, 524288], P(None, ('gx', 'gy', 'gz')), may hold values from -6 to 6
- stress: float32 [9, 524288], P(None, ('gx', 'gy', 'gz')), may hold values from -6 to 6
- mass: float32 [524288], P(('gx', 'gy', 'gz')), may hold values from 0.3 to 3
- block_tile: int32 [4096], P(('gx', 'gy', 'gz')), may hold values from 0 to 127
- live_blocks: int32 [256], P(('gx', 'gy', 'gz')), may hold values from 2 to 16, as said below
- bucket_mask: int32 [16, 128, 1024], P('gz', 'gx', 'gy'), may hold values from 0 to 2
- friction_class: int32 [16, 128, 1024], P('gz', 'gx', 'gy'), may hold values from 0 to 3
- bucket_velocity: float32 [3], replicated, may hold values from -4 to 4
Outputs:
- new_velocity: float32 [3, 524288], P(None, ('gx', 'gy', 'gz'))
- new_affine: float32 [9, 524288], P(None, ('gx', 'gy', 'gz'))
- new_offsets: float32 [3, 524288], P(None, ('gx', 'gy', 'gz'))
Inputs may be any that keep to these rules, and one draw needn't show every extreme that they name: `block_tile`: tile numbers count tiles of 4 x 4 x 4 nodes of one device's block, z slowest, y fastest: there are 1, 4 and 32 of them along z, x and y. cells[p] = 16 a + 4 b + c puts particle p's nearest node at (a, b, c) inside the tile of its block. Blocks of a device at positions live_blocks and beyond hold no particles; some device has all 16 blocks live.
All inputs are finite; a program needn't handle non-finite values.
Results may differ from a plain program's by a relative error of at most 0.00028.
Values sent between devices are 32-bit elements; how exact they have to be, the bound alone decides.
A program may use at most 64 MiB of HBM per device.

v0:
```python
import math

import jax
import jax.numpy as jnp
from jax import lax
from jax.sharding import PartitionSpec as P

DT = 0.1
GRAVITY = -9.8
MASS_FLOOR = 0.5
SLIP_FLOOR = 0.1
FRICTION = (0.1, 0.4, 0.8, 1.2)


def extended(block, sides, width, periodic):
    for axis, dim in sides:
        count = lax.axis_size(axis)
        forward = [(i, i + 1) for i in range(count - 1)]
        if periodic:
            forward.append((count - 1, 0))
        backward = [(target, source) for source, target in forward]
        low = lax.ppermute(
            lax.slice_in_dim(block, block.shape[dim] - width, None, axis=dim), axis, forward
        )
        high = lax.ppermute(lax.slice_in_dim(block, 0, width, axis=dim), axis, backward)
        block = jnp.concatenate([low, block, high], axis=dim)
    return block


def spline_axis(near, frac):
    ext = jnp.arange(6, dtype=jnp.int32)
    near = near[..., None]
    frac = frac[..., None]
    first = 0.5 * (1.5 - frac) * (1.5 - frac)
    middle = 0.75 - (frac - 1.0) * (frac - 1.0)
    last = 0.5 * (frac - 0.5) * (frac - 0.5)
    return (
        jnp.where(ext == near, first, 0.0)
        + jnp.where(ext == near + 1, middle, 0.0)
        + jnp.where(ext == near + 2, last, 0.0)
    )


def spline_matrix(near, frac):
    depth_weight = spline_axis(near[:, 0], frac[:, 0])
    row_w = spline_axis(near[:, 1], frac[:, 1])
    col_w = spline_axis(near[:, 2], frac[:, 2])
    full = (
        depth_weight[:, :, :, None, None] * row_w[:, :, None, :, None] * col_w[:, :, None, None, :]
    )
    return full.reshape(full.shape[0], full.shape[1], 216)


def node_coords():
    ident = jnp.arange(216, dtype=jnp.int32)
    return jnp.stack([ident // 36, ident // 6 % 6, ident % 6]).astype(jnp.float32)


def scatter_group(pieces):
    near, frac, moving, push, twist = pieces
    group = near.shape[0]
    square_array = spline_matrix(near, frac)
    shift = near.astype(jnp.float32) + frac
    linear = moving[:, None] * push - jnp.sum(
        twist.reshape(group, 3, 3, 128) * shift[:, None], axis=2
    )
    column_list = jnp.concatenate([moving[:, None], linear, twist], axis=1)
    block_patch = jnp.einsum(
        "yum,ymi->yui", column_list, square_array, precision=lax.Precision.HIGHEST
    )
    coords = node_coords()
    moment = block_patch[:, 1:4] + jnp.sum(
        block_patch[:, 4:13].reshape(group, 3, 3, 216) * coords[None, None], axis=2
    )
    return jnp.concatenate([block_patch[:, 0:1], moment], axis=1)


def fold_pair(arr, axis):
    count = arr.shape[axis]
    shape = arr.shape[:axis] + (count * 4,) + arr.shape[axis + 2 :]
    head = lax.slice_in_dim(arr, 0, 4, axis=axis + 1).reshape(shape)
    tail = lax.slice_in_dim(arr, 4, 6, axis=axis + 1)
    tail = jnp.concatenate([tail, jnp.zeros_like(tail)], axis=axis + 1).reshape(shape)
    pads_head = [(0, 0)] * len(shape)
    pads_tail = [(0, 0)] * len(shape)
    pads_head[axis] = (0, 4)
    pads_tail[axis] = (4, 0)
    joined = jnp.pad(head, pads_head) + jnp.pad(tail, pads_tail)
    return lax.slice_in_dim(joined, 0, count * 4 + 2, axis=axis)


def edge_layers(grid, dim):
    size = grid.shape[dim]
    return jnp.concatenate(
        [lax.slice_in_dim(grid, 0, 1, axis=dim), lax.slice_in_dim(grid, size - 1, size, axis=dim)],
        axis=dim,
    )


def split_rims(grid, dim):
    size = grid.shape[dim]
    return (edge_layers(grid, dim), lax.slice_in_dim(grid, 1, size - 1, axis=dim))


def add_rims(inner, wide, dim):
    size = inner.shape[dim]
    low = lax.slice_in_dim(wide, 0, 1, axis=dim)
    high = lax.slice_in_dim(wide, 3, 4, axis=dim)
    pads_low = [(0, 0)] * inner.ndim
    pads_high = [(0, 0)] * inner.ndim
    pads_low[dim] = (0, size - 1)
    pads_high[dim] = (size - 1, 0)
    return inner + jnp.pad(low, pads_low) + jnp.pad(high, pads_high)


def attach_ghosts(grid, wide, dim):
    low = lax.slice_in_dim(wide, 0, 1, axis=dim)
    high = lax.slice_in_dim(wide, 3, 4, axis=dim)
    return jnp.concatenate([low, grid, high], axis=dim)


def fold_x(grid):
    rims, inner = split_rims(grid, 2)
    wide = extended(rims, (("gx", 2),), 1, True)
    return add_rims(inner, wide, 2)


def fold_y(grid):
    rims, inner = split_rims(grid, 3)
    wide = extended(rims, (("gy", 3),), 1, True)
    return add_rims(inner, wide, 3)


def fold_z(grid):
    rims, inner = split_rims(grid, 1)
    wide = extended(rims, (("gz", 1),), 1, False)
    return add_rims(inner, wide, 1)


def ghost_x(grid):
    wide = extended(edge_layers(grid, 2), (("gx", 2),), 1, True)
    return attach_ghosts(grid, wide, 2)


def ghost_y(grid):
    wide = extended(edge_layers(grid, 3), (("gy", 3),), 1, True)
    return attach_ghosts(grid, wide, 3)


def ghost_z(grid):
    wide = extended(edge_layers(grid, 1), (("gz", 1),), 1, False)
    return attach_ghosts(grid, wide, 1)


def grid_update(summed, bucket_mask, friction_class, bucket_velocity):
    speed = summed[1:4] / jnp.maximum(summed[0], MASS_FLOOR)[None]
    speed = jnp.concatenate([speed[0:1] + DT * GRAVITY, speed[1:3]], axis=0)
    coeff = jnp.zeros(friction_class.shape, jnp.float32)
    for level in range(4):
        coeff = coeff + jnp.where(friction_class == level, FRICTION[level], 0.0)
    bvel = bucket_velocity.reshape(3, 1, 1, 1)
    rel = speed - bvel
    normal = jnp.minimum(rel[0], 0.0)
    slide = jnp.sqrt(rel[1] * rel[1] + rel[2] * rel[2])
    multiplier = jnp.maximum(0.0, 1.0 + coeff * normal / jnp.maximum(slide, SLIP_FLOOR))
    contact = bvel + jnp.stack([rel[0] - normal, multiplier * rel[1], multiplier * rel[2]])
    final_output = jnp.where((bucket_mask == 1)[None], contact, speed)
    return jnp.where((bucket_mask == 2)[None], jnp.broadcast_to(bvel, speed.shape), final_output)


def on_device(
    cells,
    offsets,
    velocity,
    affine,
    stress,
    mass,
    block_tile,
    live_blocks,
    bucket_mask,
    friction_class,
    bucket_velocity,
):
    depth, rows, width = bucket_mask.shape
    blocks = block_tile.shape[0]
    group = math.gcd(blocks, 32)
    rounds = blocks // group
    tiles_z = depth // 4
    tiles_x = rows // 4
    tiles_y = width // 4
    alive = (jnp.arange(blocks, dtype=jnp.int32) < live_blocks[0]).astype(jnp.float32)
    within = cells.reshape(blocks, 128)
    near = jnp.stack([within // 16, within // 4 % 4, within % 4], axis=1)
    frac = offsets.reshape(3, blocks, 128).transpose(1, 0, 2)
    anchor = jnp.stack(
        [
            block_tile // (tiles_x * tiles_y) * 4,
            block_tile // tiles_y % tiles_x * 4,
            block_tile % tiles_y * 4,
        ],
        axis=1,
    )
    moving = mass.reshape(blocks, 128) * alive[:, None]
    push = velocity.reshape(3, blocks, 128).transpose(1, 0, 2)
    twist = (mass[None] * affine - 4.0 * DT * stress).reshape(9, blocks, 128).transpose(
        1, 0, 2
    ) * alive[:, None, None]

    def batched(arr):
        return arr.reshape((rounds, group) + arr.shape[1:])

    tiles = lax.map(
        scatter_group,
        (batched(near), batched(frac), batched(moving), batched(push), batched(twist)),
    )
    tiles = tiles.reshape(blocks, 4, 216)
    summed = jax.ops.segment_sum(tiles, block_tile, num_segments=tiles_z * tiles_x * tiles_y)
    grid = summed.reshape(tiles_z, tiles_x, tiles_y, 4, 6, 6, 6).transpose(3, 0, 4, 1, 5, 2, 6)
    grid = fold_pair(grid, 1)
    grid = fold_pair(grid, 2)
    grid = fold_pair(grid, 3)
    grid = fold_x(grid)
    grid = fold_y(grid)
    grid = fold_z(grid)
    speed = grid_update(grid, bucket_mask, friction_class, bucket_velocity)
    padded = ghost_z(ghost_y(ghost_x(speed)))

    def gather_group(pieces):
        part_near, part_frac, part_anchor, part_alive = pieces
        count = part_near.shape[0]
        square_array = spline_matrix(part_near, part_frac)

        def cut(start):
            return lax.dynamic_slice(padded, (0, start[0], start[1], start[2]), (3, 6, 6, 6))

        nodal = jax.vmap(cut)(part_anchor).reshape(count, 3, 216)
        coords = node_coords()
        spread = (nodal[:, :, None, :] * coords[None, None]).reshape(count, 9, 216)
        lookup_grid = jnp.concatenate([nodal, spread], axis=1)
        final_output = jnp.einsum(
            "lzr,lor->lzo", lookup_grid, square_array, precision=lax.Precision.HIGHEST
        )
        moved = final_output[:, 0:3]
        shift = part_near.astype(jnp.float32) + part_frac
        bend = final_output[:, 3:12].reshape(count, 3, 3, 128) - moved[:, :, None] * shift[:, None]
        flag = part_alive[:, None, None]
        return (
            moved * flag,
            4.0 * bend.reshape(count, 9, 128) * flag,
            (part_frac + DT * moved) * flag,
        )

    moved, bent, shifted = lax.map(
        gather_group, (batched(near), batched(frac), batched(anchor), batched(alive))
    )
    new_velocity = moved.reshape(blocks, 3, 128).transpose(1, 0, 2).reshape(3, blocks * 128)
    new_affine = bent.reshape(blocks, 9, 128).transpose(1, 0, 2).reshape(9, blocks * 128)
    new_offsets = shifted.reshape(blocks, 3, 128).transpose(1, 0, 2).reshape(3, blocks * 128)
    return (new_velocity, new_affine, new_offsets)


def solution(mesh):
    return jax.shard_map(
        on_device,
        mesh=mesh,
        in_specs=(
            P(("gx", "gy", "gz")),
            P(None, ("gx", "gy", "gz")),
            P(None, ("gx", "gy", "gz")),
            P(None, ("gx", "gy", "gz")),
            P(None, ("gx", "gy", "gz")),
            P(("gx", "gy", "gz")),
            P(("gx", "gy", "gz")),
            P(("gx", "gy", "gz")),
            P("gz", "gx", "gy"),
            P("gz", "gx", "gy"),
            P(),
        ),
        out_specs=(
            P(None, ("gx", "gy", "gz")),
            P(None, ("gx", "gy", "gz")),
            P(None, ("gx", "gy", "gz")),
        ),
        check_vma=False,
    )
```

profile of v0, /device:TPU:71, one launch (start us, length us, event | category | flops | bytes accessed | tf_op | source)
XLA Modules:
  0.0 107.9 jit_solution(15966507643463367874)
XLA Ops:
  7.8 3.1 %fusion.2 = f32[16,13,216]{2,1,0:T(8,128)S(1)} fusion(f32[16,128,216]{1,0,2:T(8,128)S(1)} %bitcast.158, f32[16,13,128]{2,0,1:T(8,128)S(1)} %pad_maximum_fusion.3), kind=kOutput, calls=%fused_computation.9 | convolution fusion | flops 69009408 | bytes 2055680 | tf_op jit(solution)/shard_map/while/body/eval_jaxpr/yum,ymi->yui/dot_general | solution.py:68
  13.4 1.9 %reshape.794 = f32[1,4,32,4,6,6,6]{2,1,6,5,4,3,0:T(4,128)S(1)} reshape(f32[128,4,216]{0,2,1:T(8,128)} %copy.291) | data formatting | bytes 884736 | tf_op jit(solution)/shard_map/reshape | solution.py:218
  17.2 1.3 %fusion.4 = f32[4,6,18,32,4]{3,2,4,1,0:T(8,128)} fusion(f32[4,6,16,32,6]{3,2,4,1,0:T(8,128)S(1)} %bitcast.163, f32[4,6,16,32,6]{3,2,4,1,0:T(8,128)S(1)} %bitcast.161), kind=kLoop, calls=%fused_computation.11 | loop fusion | flops 55296 | bytes 811008 | tf_op jit(solution)/shard_map/add | solution.py:88
  18.5 1.3 %copy.319 = f32[4,6,18,32,2]{2,4,3,1,0:T(2,128)} copy(f32[4,6,18,32,2]{3,2,4,1,0:T(8,128)S(1)} %pad_add_fusion) | data formatting | bytes 221184
  19.8 1.5 %concatenate.45.clone = f32[4,6,18,32,4]{2,4,3,1,0:T(4,128)S(1)} pad(f32[4,6,18,32,2]{2,4,3,1,0:T(2,128)} %copy.319, f32[]{:T(128)} %constant.217.clone.1), padding=0_0x0_0x0_0x0_0x0_2 | pad | bytes 331780 | tf_op jit(solution)/shard_map/concatenate | solution.py:83
  21.3 1.2 %copy.297 = f32[4,6,18,128]{3,2,1,0:T(8,128)} copy(f32[4,6,18,128]{2,3,1,0:T(8,128)S(1)} %bitcast.166) | data formatting | bytes 442368 | tf_op jit(solution)/shard_map/reshape | solution.py:83
  22.4 1.8 %copy.294 = f32[4,6,18,32,4]{2,4,3,1,0:T(4,128)S(1)} copy(f32[4,6,18,32,4]{3,2,4,1,0:T(8,128)} %fusion.4) | data formatting | bytes 442368 | tf_op jit(solution)/shard_map/slice | solution.py:81
  24.3 1.2 %copy.295 = f32[4,6,18,128]{3,2,1,0:T(8,128)} copy(f32[4,6,18,128]{2,3,1,0:T(8,128)S(1)} %bitcast.167) | data formatting | bytes 442368 | tf_op jit(solution)/shard_map/reshape | solution.py:81
  25.5 1.2 %fusion.26 = (f32[4,6,1,130]{3,2,1,0:T(1,128)S(1)}, f32[4,6,1,130]{3,2,1,0:T(1,128)S(1)}) fusion(f32[4,6,18,128]{3,2,1,0:T(8,128)} %copy.295, f32[4,6,18,128]{3,2,1,0:T(8,128)} %copy.297), kind=kLoop, calls=%fused_computation.89 | loop fusion | flops 6240 | bytes 467328 | tf_op jit(solution)/shard_map/add | solution.py:88
  26.7 1.3 %collective-permute-start = (f32[4,6,1,130]{3,0,2,1:T(4,128)S(1)}, f32[4,6,1,130]{3,0,2,1:T(4,128)S(1)}, u32[]{:S(2)}, u32[]{:S(2)}) collective-permute-start(f32[4,6,1,130]{3,0,2,1:T(4,128)S(1)} %copy.298), channel_id=1, source_target_pairs={{0,32},{32,64},{64,96},{96,128},{128,160},{160,192},{192,224},{224... | collective-permute-start | bytes 37448 | tf_op jit(solution)/shard_map/ppermute | solution.py:22
  28.2 1.2 %collective-permute-done = f32[4,6,1,130]{3,0,2,1:T(4,128)S(1)} collective-permute-done((f32[4,6,1,130]{3,0,2,1:T(4,128)S(1)}, f32[4,6,1,130]{3,0,2,1:T(4,128)S(1)}, u32[]{:S(2)}, u32[]{:S(2)}) %collective-permute-start) | collective-permute-done | bytes 12512 | tf_op jit(solution)/shard_map/ppermute | solution.py:22
  29.5 3.3 %collective-permute-done.1 = f32[4,6,1,130]{3,0,2,1:T(4,128)S(1)} collective-permute-done((f32[4,6,1,130]{3,0,2,1:T(4,128)S(1)}, f32[4,6,1,130]{3,0,2,1:T(4,128)S(1)}, u32[]{:S(2)}, u32[]{:S(2)}) %collective-permute-start.1) | collective-permute-done | bytes 12512 | tf_op jit(solution)/shard_map/ppermute | solution.py:25
  32.8 1.2 %fusion.8 = f32[4,6,16,130]{3,2,1,0:T(8,128)S(1)} fusion(f32[4,6,18,128]{3,2,1,0:T(8,128)} %copy.295, f32[4,6,18,128]{3,2,1,0:T(8,128)} %copy.297, f32[4,6,1,130]{3,2,1,0:T(1,128)S(1)} %copy.301, f32[4,6,1,130]{3,2,1,0:T(1,128)S(1)} %copy.299), kind=kLoop, calls=%fused_computation.24 | loop fusion | flops 149760 | bytes 667008 | tf_op jit(solution)/shard_map/add | solution.py:113
  34.2 1.7 %collective-permute-start.2 = (f32[4,6,16,1]{3,2,1,0:T(8,128)S(1)}, f32[4,6,16,1]{3,2,1,0:T(8,128)S(1)}, u32[]{:S(2)}, u32[]{:S(2)}) collective-permute-start(f32[4,6,16,1]{3,2,1,0:T(8,128)S(1)} %get-tuple-element.48), channel_id=1, source_target_pairs={{0,4},{4,8},{8,12},{12,16},{16,20},{20,24},{24,28},{28,0},{1,5},{5... | collective-permute-start | bytes 4616 | tf_op jit(solution)/shard_map/ppermute | solution.py:22
  35.9 2.9 %collective-permute-done.2 = f32[4,6,16,1]{3,2,1,0:T(8,128)S(1)} collective-permute-done((f32[4,6,16,1]{3,2,1,0:T(8,128)S(1)}, f32[4,6,16,1]{3,2,1,0:T(8,128)S(1)}, u32[]{:S(2)}, u32[]{:S(2)}) %collective-permute-start.2) | collective-permute-done | bytes 1568 | tf_op jit(solution)/shard_map/ppermute | solution.py:22
  38.8 3.0 %collective-permute-done.3 = f32[4,6,16,1]{3,2,1,0:T(8,128)S(1)} collective-permute-done((f32[4,6,16,1]{3,2,1,0:T(8,128)S(1)}, f32[4,6,16,1]{3,2,1,0:T(8,128)S(1)}, u32[]{:S(2)}, u32[]{:S(2)}) %collective-permute-start.3) | collective-permute-done | bytes 1568 | tf_op jit(solution)/shard_map/ppermute | solution.py:25
  42.0 7.7 %collective-permute-start.4 = (f32[4,1,16,128]{3,2,1,0:T(8,128)S(1)}, f32[4,1,16,128]{3,2,1,0:T(8,128)S(1)}, u32[]{:S(2)}, u32[]{:S(2)}) collective-permute-start(f32[4,1,16,128]{3,2,1,0:T(8,128)S(1)} %get-tuple-element.52), channel_id=1, source_target_pairs={{0,1},{1,2},{2,3},{4,5},{5,6},{6,7},{8,9},{9,10},{10,11},{12,13},{... | collective-permute-start | bytes 98312 | tf_op jit(solution)/shard_map/ppermute | solution.py:22
  49.7 2.1 %collective-permute-start.5 = (f32[4,1,16,128]{3,2,1,0:T(8,128)S(1)}, f32[4,1,16,128]{3,2,1,0:T(8,128)S(1)}, u32[]{:S(2)}, u32[]{:S(2)}) collective-permute-start(f32[4,1,16,128]{3,2,1,0:T(8,128)S(1)} %get-tuple-element.53), channel_id=1, source_target_pairs={{1,0},{2,1},{3,2},{5,4},{6,5},{7,6},{9,8},{10,9},{11,10},{13,12},{... | collective-permute-start | bytes 98312 | tf_op jit(solution)/shard_map/ppermute | solution.py:25
  51.8 4.6 %collective-permute-done.5 = f32[4,1,16,128]{3,2,1,0:T(8,128)S(1)} collective-permute-done((f32[4,1,16,128]{3,2,1,0:T(8,128)S(1)}, f32[4,1,16,128]{3,2,1,0:T(8,128)S(1)}, u32[]{:S(2)}, u32[]{:S(2)}) %collective-permute-start.5) | collective-permute-done | bytes 32800 | tf_op jit(solution)/shard_map/ppermute | solution.py:25
  56.9 1.5 %collective-permute-start.7 = (f32[3,4,1,128]{3,2,1,0:T(1,128)S(1)}, f32[3,4,1,128]{3,2,1,0:T(1,128)S(1)}, u32[]{:S(2)}, u32[]{:S(2)}) collective-permute-start(f32[3,4,1,128]{3,2,1,0:T(1,128)S(1)} %get-tuple-element.69), channel_id=1, source_target_pairs={{32,0},{64,32},{96,64},{128,96},{160,128},{192,160},{224,192},{0,2... | collective-permute-start | bytes 18440 | tf_op jit(solution)/shard_map/ppermute | solution.py:25
  59.3 2.2 %collective-permute-done.7 = f32[3,4,1,128]{3,2,1,0:T(1,128)S(1)} collective-permute-done((f32[3,4,1,128]{3,2,1,0:T(1,128)S(1)}, f32[3,4,1,128]{3,2,1,0:T(1,128)S(1)}, u32[]{:S(2)}, u32[]{:S(2)}) %collective-permute-start.7) | collective-permute-done | bytes 6176 | tf_op jit(solution)/shard_map/ppermute | solution.py:25
  61.7 3.0 %collective-permute-start.8 = (f32[3,4,18,1]{3,1,2,0:T(4,128)S(1)}, f32[3,4,18,1]{3,1,2,0:T(4,128)S(1)}, u32[]{:S(2)}, u32[]{:S(2)}) collective-permute-start(f32[3,4,18,1]{3,1,2,0:T(4,128)S(1)} %get-tuple-element.66), channel_id=1, source_target_pairs={{0,4},{4,8},{8,12},{12,16},{16,20},{20,24},{24,28},{28,0},{1,5},{5... | collective-permute-start | bytes 2600 | tf_op jit(solution)/shard_map/ppermute | solution.py:22
  64.7 1.7 %collective-permute-done.8 = f32[3,4,18,1]{3,1,2,0:T(4,128)S(1)} collective-permute-done((f32[3,4,18,1]{3,1,2,0:T(4,128)S(1)}, f32[3,4,18,1]{3,1,2,0:T(4,128)S(1)}, u32[]{:S(2)}, u32[]{:S(2)}) %collective-permute-start.8) | collective-permute-done | bytes 896 | tf_op jit(solution)/shard_map/ppermute | solution.py:22
  66.5 1.8 %collective-permute-done.9 = f32[3,4,18,1]{3,1,2,0:T(4,128)S(1)} collective-permute-done((f32[3,4,18,1]{3,1,2,0:T(4,128)S(1)}, f32[3,4,18,1]{3,1,2,0:T(4,128)S(1)}, u32[]{:S(2)}, u32[]{:S(2)}) %collective-permute-start.9) | collective-permute-done | bytes 896 | tf_op jit(solution)/shard_map/ppermute | solution.py:25
  68.6 4.5 %collective-permute-start.10 = (f32[3,1,18,130]{3,1,2,0:T(1,128)S(1)}, f32[3,1,18,130]{3,1,2,0:T(1,128)S(1)}, u32[]{:S(2)}, u32[]{:S(2)}) collective-permute-start(f32[3,1,18,130]{3,1,2,0:T(1,128)S(1)} %get-tuple-element.50), channel_id=1, source_target_pairs={{0,1},{1,2},{2,3},{4,5},{5,6},{6,7},{8,9},{9,10},{10,11},{12,13},{... | collective-permute-start | bytes 84248 | tf_op jit(solution)/shard_map/ppermute | solution.py:22
  73.1 1.9 %collective-permute-start.11 = (f32[3,1,18,130]{3,1,2,0:T(1,128)S(1)}, f32[3,1,18,130]{3,1,2,0:T(1,128)S(1)}, u32[]{:S(2)}, u32[]{:S(2)}) collective-permute-start(f32[3,1,18,130]{3,1,2,0:T(1,128)S(1)} %get-tuple-element.51), channel_id=1, source_target_pairs={{1,0},{2,1},{3,2},{5,4},{6,5},{7,6},{9,8},{10,9},{11,10},{13,12},{... | collective-permute-start | bytes 84248 | tf_op jit(solution)/shard_map/ppermute | solution.py:25
  75.1 4.5 %copy.306 = f32[3,4,18,130]{1,0,3,2:T(4,128)} copy(f32[3,4,18,130]{3,1,2,0:T(4,128)S(1)} %pad_maximum_fusion.1) | data formatting | bytes 224640 | tf_op jit(solution)/shard_map/concatenate | solution.py:119
  79.7 4.5 %copy.305 = f32[3,1,18,130]{1,0,3,2:T(4,128)} copy(f32[3,1,18,130]{3,1,2,0:T(1,128)S(1)} %collective-permute-done.10) | data formatting | bytes 56160 | tf_op jit(solution)/shard_map/ppermute | solution.py:22
  84.2 4.5 %copy.307 = f32[3,1,18,130]{1,0,3,2:T(4,128)} copy(f32[3,1,18,130]{3,1,2,0:T(1,128)S(1)} %collective-permute-done.11) | data formatting | bytes 56160 | tf_op jit(solution)/shard_map/ppermute | solution.py:25
  88.7 10.5 %pad_maximum_fusion = f32[3,6,18,130]{1,0,3,2:T(4,128)} fusion(f32[3,1,18,130]{1,0,3,2:T(4,128)} %copy.307, f32[3,4,18,130]{1,0,3,2:T(4,128)} %copy.306, f32[3,1,18,130]{1,0,3,2:T(4,128)} %copy.305), kind=kLoop, calls=%fused_computation.2 | loop fusion | flops 84240 | bytes 336960 | tf_op jit(solution)/shard_map/concatenate | solution.py:119
  99.2 3.6 %gather_fusion = f32[16,3,6,6,6]{2,1,4,3,0:T(4,128)S(1)} fusion(f32[3,6,18,130]{1,0,3,2:T(4,128)} %pad_maximum_fusion, s32[16]{0:T(128)S(1)} %fusion.42), kind=kCustom, calls=%fused_computation | custom fusion | bytes 83200 | tf_op jit(solution)/shard_map/while/body/eval_jaxpr/vmap()/gather | solution.py:234
  104.4 2.0 %fusion = f32[16,12,128]{2,1,0:T(8,128)S(1)} fusion(f32[16,128,216]{1,0,2:T(8,128)S(1)} %bitcast.159, f32[16,9,216]{2,1,0:T(8,128)S(1)} %copy_multiply_fusion, f32[16,3,216]{2,1,0:T(4,128)S(1)} %copy.311), kind=kOutput, calls=%fused_computation.7 | convolution fusion | flops 63742464 | bytes 2033664 | tf_op jit(solution)/shard_map/while/body/eval_jaxpr/lzr,lor->lzo/dot_general | solution.py:240
  (114 shorter events, 16.2 us)
Async XLA Ops:
  4.1 3.7 %copy-start.4 = (f32[3,2048]{1,0:T(4,128)S(1)}, f32[3,2048]{1,0:T(4,128)}, u32[]{:S(2)}) copy-start(f32[3,2048]{1,0:T(4,128)} %param.13) | copy-start | bytes 73732
  7.4 3.5 %copy-start.1 = (f32[16,3,128]{2,0,1:T(8,128)}, f32[16,3,128]{2,0,1:T(8,128)S(1)}, u32[]{:S(2)}) copy-start(f32[16,3,128]{2,0,1:T(8,128)S(1)} %copy.281) | copy-start | bytes 73732
  7.8 3.5 %copy-start.7 = (s32[16]{0:T(128)S(1)}, s32[16]{0:T(128)}, u32[]{:S(2)}) copy-start(s32[16]{0:T(128)} %param.17) | copy-start | bytes 196
  25.5 26.3 %copy-start.3 = (s32[4,16,128]{2,1,0:T(8,128)S(1)}, s32[4,16,128]{2,1,0:T(8,128)}, u32[]{:S(2)}) copy-start(s32[4,16,128]{2,1,0:T(8,128)} %param.19) | copy-start | bytes 98308
  26.7 2.8 %collective-permute-start = (f32[4,6,1,130]{3,0,2,1:T(4,128)S(1)}, f32[4,6,1,130]{3,0,2,1:T(4,128)S(1)}, u32[]{:S(2)}, u32[]{:S(2)}) collective-permute-start(f32[4,6,1,130]{3,0,2,1:T(4,128)S(1)} %copy.298), channel_id=1, source_target_pairs={{0,32},{32,64},{64,96},{96,128},{128,160},{160,192},{192,224},{224... | collective-permute-start | bytes 37448 | tf_op jit(solution)/shard_map/ppermute | solution.py:22
  28.0 4.8 %collective-permute-start.1 = (f32[4,6,1,130]{3,0,2,1:T(4,128)S(1)}, f32[4,6,1,130]{3,0,2,1:T(4,128)S(1)}, u32[]{:S(2)}, u32[]{:S(2)}) collective-permute-start(f32[4,6,1,130]{3,0,2,1:T(4,128)S(1)} %copy.300), channel_id=1, source_target_pairs={{32,0},{64,32},{96,64},{128,96},{160,128},{192,160},{224,192},{0,2... | collective-permute-start | bytes 37448 | tf_op jit(solution)/shard_map/ppermute | solution.py:25
  32.8 23.7 %copy-start.6 = (f32[3]{0:T(128)S(1)}, f32[3]{0:T(128)}, u32[]{:S(2)}) copy-start(f32[3]{0:T(128)} %param.21) | copy-start | bytes 40
  32.8 23.8 %copy-start.5 = (s32[4,16,128]{2,1,0:T(8,128)S(1)}, s32[4,16,128]{2,1,0:T(8,128)}, u32[]{:S(2)}) copy-start(s32[4,16,128]{2,1,0:T(8,128)} %param.20) | copy-start | bytes 98308
  34.2 4.6 %collective-permute-start.2 = (f32[4,6,16,1]{3,2,1,0:T(8,128)S(1)}, f32[4,6,16,1]{3,2,1,0:T(8,128)S(1)}, u32[]{:S(2)}, u32[]{:S(2)}) collective-permute-start(f32[4,6,16,1]{3,2,1,0:T(8,128)S(1)} %get-tuple-element.48), channel_id=1, source_target_pairs={{0,4},{4,8},{8,12},{12,16},{16,20},{20,24},{24,28},{28,0},{1,5},{5... | collective-permute-start | bytes 4616 | tf_op jit(solution)/shard_map/ppermute | solution.py:22
  35.9 5.9 %collective-permute-start.3 = (f32[4,6,16,1]{3,2,1,0:T(8,128)S(1)}, f32[4,6,16,1]{3,2,1,0:T(8,128)S(1)}, u32[]{:S(2)}, u32[]{:S(2)}) collective-permute-start(f32[4,6,16,1]{3,2,1,0:T(8,128)S(1)} %get-tuple-element.49), channel_id=1, source_target_pairs={{4,0},{8,4},{12,8},{16,12},{20,16},{24,20},{28,24},{0,28},{5,1},{9... | collective-permute-start | bytes 4616 | tf_op jit(solution)/shard_map/ppermute | solution.py:25
  42.0 9.8 %collective-permute-start.4 = (f32[4,1,16,128]{3,2,1,0:T(8,128)S(1)}, f32[4,1,16,128]{3,2,1,0:T(8,128)S(1)}, u32[]{:S(2)}, u32[]{:S(2)}) collective-permute-start(f32[4,1,16,128]{3,2,1,0:T(8,128)S(1)} %get-tuple-element.52), channel_id=1, source_target_pairs={{0,1},{1,2},{2,3},{4,5},{5,6},{6,7},{8,9},{9,10},{10,11},{12,13},{... | collective-permute-start | bytes 98312 | tf_op jit(solution)/shard_map/ppermute | solution.py:22
  49.7 6.7 %collective-permute-start.5 = (f32[4,1,16,128]{3,2,1,0:T(8,128)S(1)}, f32[4,1,16,128]{3,2,1,0:T(8,128)S(1)}, u32[]{:S(2)}, u32[]{:S(2)}) collective-permute-start(f32[4,1,16,128]{3,2,1,0:T(8,128)S(1)} %get-tuple-element.53), channel_id=1, source_target_pairs={{1,0},{2,1},{3,2},{5,4},{6,5},{7,6},{9,8},{10,9},{11,10},{13,12},{... | collective-permute-start | bytes 98312 | tf_op jit(solution)/shard_map/ppermute | solution.py:25
  56.8 2.6 %collective-permute-start.6 = (f32[3,4,1,128]{3,2,1,0:T(1,128)S(1)}, f32[3,4,1,128]{3,2,1,0:T(1,128)S(1)}, u32[]{:S(2)}, u32[]{:S(2)}) collective-permute-start(f32[3,4,1,128]{3,2,1,0:T(1,128)S(1)} %get-tuple-element.68), channel_id=1, source_target_pairs={{0,32},{32,64},{64,96},{96,128},{128,160},{160,192},{192,224},{224... | collective-permute-start | bytes 18440 | tf_op jit(solution)/shard_map/ppermute | solution.py:22
  56.9 4.7 %collective-permute-start.7 = (f32[3,4,1,128]{3,2,1,0:T(1,128)S(1)}, f32[3,4,1,128]{3,2,1,0:T(1,128)S(1)}, u32[]{:S(2)}, u32[]{:S(2)}) collective-permute-start(f32[3,4,1,128]{3,2,1,0:T(1,128)S(1)} %get-tuple-element.69), channel_id=1, source_target_pairs={{32,0},{64,32},{96,64},{128,96},{160,128},{192,160},{224,192},{0,2... | collective-permute-start | bytes 18440 | tf_op jit(solution)/shard_map/ppermute | solution.py:25
  61.7 4.8 %collective-permute-start.8 = (f32[3,4,18,1]{3,1,2,0:T(4,128)S(1)}, f32[3,4,18,1]{3,1,2,0:T(4,128)S(1)}, u32[]{:S(2)}, u32[]{:S(2)}) collective-permute-start(f32[3,4,18,1]{3,1,2,0:T(4,128)S(1)} %get-tuple-element.66), channel_id=1, source_target_pairs={{0,4},{4,8},{8,12},{12,16},{16,20},{20,24},{24,28},{28,0},{1,5},{5... | collective-permute-start | bytes 2600 | tf_op jit(solution)/shard_map/ppermute | solution.py:22
  64.7 3.6 %collective-permute-start.9 = (f32[3,4,18,1]{3,1,2,0:T(4,128)S(1)}, f32[3,4,18,1]{3,1,2,0:T(4,128)S(1)}, u32[]{:S(2)}, u32[]{:S(2)}) collective-permute-start(f32[3,4,18,1]{3,1,2,0:T(4,128)S(1)} %get-tuple-element.67), channel_id=1, source_target_pairs={{4,0},{8,4},{12,8},{16,12},{20,16},{24,20},{28,24},{0,28},{5,1},{9... | collective-permute-start | bytes 2600 | tf_op jit(solution)/shard_map/ppermute | solution.py:25
  68.6 11.0 %collective-permute-start.10 = (f32[3,1,18,130]{3,1,2,0:T(1,128)S(1)}, f32[3,1,18,130]{3,1,2,0:T(1,128)S(1)}, u32[]{:S(2)}, u32[]{:S(2)}) collective-permute-start(f32[3,1,18,130]{3,1,2,0:T(1,128)S(1)} %get-tuple-element.50), channel_id=1, source_target_pairs={{0,1},{1,2},{2,3},{4,5},{5,6},{6,7},{8,9},{9,10},{10,11},{12,13},{... | collective-permute-start | bytes 84248 | tf_op jit(solution)/shard_map/ppermute | solution.py:22
  73.1 11.0 %collective-permute-start.11 = (f32[3,1,18,130]{3,1,2,0:T(1,128)S(1)}, f32[3,1,18,130]{3,1,2,0:T(1,128)S(1)}, u32[]{:S(2)}, u32[]{:S(2)}) collective-permute-start(f32[3,1,18,130]{3,1,2,0:T(1,128)S(1)} %get-tuple-element.51), channel_id=1, source_target_pairs={{1,0},{2,1},{3,2},{5,4},{6,5},{7,6},{9,8},{10,9},{11,10},{13,12},{... | collective-permute-start | bytes 84248 | tf_op jit(solution)/shard_map/ppermute | solution.py:25
  104.0 2.4 %copy-start = (f32[3,2048]{1,0:T(4,128)S(1)}, f32[3,2048]{1,0:T(4,128)}, u32[]{:S(2)}) copy-start(f32[3,2048]{1,0:T(4,128)} %param.12) | copy-start | bytes 73732
  104.1 3.0 %copy-start.2 = (f32[16,3,128]{2,0,1:T(8,128)S(1)}, f32[16,3,128]{2,0,1:T(8,128)}, u32[]{:S(2)}) copy-start(f32[16,3,128]{2,0,1:T(8,128)} %copy-done.1) | copy-start | bytes 73732
where the time goes:
time: 109 us; the launch traced here: 108 us
  local copies, waits for them, and re-layouts  31.2 us (29%)
  other arithmetic  24 us (22%)
  starting transfers between devices  24 us (22%)
  waiting for transfers between devices  21.7 us (20%)
  matrix products  5.03 us (5%)
  between operations  1.95 us (2%)
    ppermute x6, starting transfers between devices, extended(): lax.ppermute(lax.slice_in_dim(block, block.shape[dim] - width, None, axis...  18.3 us
    ppermute x6, waiting for transfers between devices, extended(): lax.ppermute(lax.slice_in_dim(block, 0, width, axis=dim), axis, backward)  15 us
    concatenate x3, other arithmetic, attach_ghosts(): return jnp.concatenate([low, grid, high], axis=dim)  10.8 us
    ppermute x6, waiting for transfers between devices, extended(): lax.ppermute(lax.slice_in_dim(block, block.shape[dim] - width, None, axis...  6.79 us
    ppermute x6, starting transfers between devices, extended(): lax.ppermute(lax.slice_in_dim(block, 0, width, axis=dim), axis, backward)  5.73 us
    gather x2, local copies, waits for them, and re-layouts, cut(): lax.dynamic_slice(padded, (0, start[0], start[1], start[2]), (3, 6, 6, 6))  4.67 us
    ppermute x2, local copies, waits for them, and re-layouts, extended(): lax.ppermute(lax.slice_in_dim(block, block.shape[dim] - width, None, axis...  4.56 us
    ppermute x2, local copies, waits for them, and re-layouts, extended(): lax.ppermute(lax.slice_in_dim(block, 0, width, axis=dim), axis, backward)  4.55 us
  transfers between devices with their start and end apart: 12, of which 9 were waited for; matrix products, arithmetic and copies ran while one was open for 9% of the time, Pallas kernels for 0%

commit v1 on v0

v1 whole, which is shorter than its diff:
```python
import functools

import jax
import jax.numpy as jnp
from jax import lax
from jax.experimental import pallas as pl
from jax.experimental.pallas import tpu as pltpu
from jax.sharding import PartitionSpec as P

DT = 0.1
GRAVITY = -9.8
MASS_FLOOR = 0.5
SLIP_FLOOR = 0.1
FRICTION = (0.1, 0.4, 0.8, 1.2)

BLOCKS = 16
UNROLL = 2
XP = 20
ROWS = 3 * XP * 8
NODES = 3 * XP
F32 = jnp.float32
BF16 = jnp.bfloat16
MESH = pl.DeviceIdType.MESH

FACES = [(dz, dx) for dz in (-1, 0, 1) for dx in (-1, 0, 1) if (dz, dx) != (0, 0)]
EDGES = [
    (dz, dx, dy)
    for dz in (-1, 0, 1)
    for dx in (-1, 0, 1)
    for dy in (-1, 0, 1)
    if (dz, dx, dy) != (0, 0, 0)
]


def spline(frac):
    weights = (
        0.5 * (1.5 - frac) * (1.5 - frac),
        0.75 - (frac - 1.0) * (frac - 1.0),
        0.5 * (frac - 0.5) * (frac - 0.5),
    )
    moments = tuple(w * (float(k) - frac) for k, w in enumerate(weights))
    return weights, moments


def pick(hits, values):
    out = jnp.where(hits[2], values[2], 0.0)
    out = jnp.where(hits[1], values[1], out)
    return jnp.where(hits[0], values[0], out)


def split(value):
    high = value.astype(BF16)
    return high, (value - high.astype(F32)).astype(BF16)


def along_z(cell, frac):
    low = lax.broadcasted_iota(jnp.int32, (8, 128), 0) & 1
    near = lax.shift_right_logical(cell, 4) - low
    weights, moments = spline(frac)
    plain, moment = [], []
    for pair in range(3):
        hits = [near == 2 * pair - k for k in range(3)]
        plain.append(pick(hits, weights))
        moment.append(pick(hits, moments))
    return plain, moment


def along_x(cell, frac):
    near = lax.shift_right_logical(cell, 2) & 3
    weights, moments = spline(frac)
    hits = [near == v for v in range(4)]
    plain, moment = [], []
    for i in range(6):
        outs = []
        for values in (weights, moments):
            out = jnp.zeros((8, 128), F32)
            for k in range(3):
                if 0 <= i - k < 4:
                    out = jnp.where(hits[i - k], values[k], out)
            outs.append(out)
        plain.append(outs[0])
        moment.append(outs[1])
    return plain, moment


def along_y(cell, frac, first):
    row = lax.broadcasted_iota(jnp.int32, (8, 128), 0)
    base = (cell & 3) + (first - 1)
    weights, moments = spline(frac)
    diff = base - row
    plain, moment = [], []
    for t in range(17):
        shifted, offset = diff, 8 * t
        if t == 0:
            shifted = jnp.where(row == 0, -999, diff)
        elif t == 15:
            shifted = jnp.where(row == 7, -999, diff)
        elif t == 16:
            node = jnp.where(row == 0, -1, jnp.where(row == 1, 0, jnp.where(row == 2, 127, 128)))
            shifted, offset = jnp.where(row < 4, base - node, -999), 0
        hits = [shifted == offset - k for k in range(3)]
        plain.append(pick(hits, weights))
        moment.append(pick(hits, moments))
    zero = jnp.zeros((8, 128), F32)
    plain.append(zero)
    moment.append(zero)
    return jnp.concatenate([jnp.concatenate(plain, 0), jnp.concatenate(moment, 0)], 1)


def by_channel(parts):
    row = lax.broadcasted_iota(jnp.int32, (8, 128), 0)
    out = jnp.where(row < 6, parts[2], parts[3])
    out = jnp.where(row < 4, parts[1], out)
    return jnp.where(row < 2, parts[0], out)


def product(left, right, dims):
    left_high, left_low = split(left)
    right_high, right_low = right
    dot = functools.partial(
        lax.dot_general, dimension_numbers=(dims, ((), ())), preferred_element_type=F32
    )
    return dot(left_high, right_high) + (dot(left_low, right_high) + dot(left_high, right_low))


def contact(mass, momentum, kind, friction, bvel):
    floor = jnp.maximum(mass, MASS_FLOOR)
    speed = [momentum[0] / floor + DT * GRAVITY, momentum[1] / floor, momentum[2] / floor]
    coeff = jnp.where(friction == 3.0, FRICTION[3], 0.0)
    for level in range(3):
        coeff = jnp.where(friction == float(level), FRICTION[level], coeff)
    rel = [speed[i] - bvel[i] for i in range(3)]
    normal = jnp.minimum(rel[0], 0.0)
    slide = jnp.sqrt(rel[1] * rel[1] + rel[2] * rel[2])
    factor = jnp.maximum(0.0, 1.0 + coeff * normal / jnp.maximum(slide, SLIP_FLOOR))
    hit = [bvel[0] + (rel[0] - normal), bvel[1] + factor * rel[1], bvel[2] + factor * rel[2]]
    return [
        jnp.where(kind == 2.0, bvel[i], jnp.where(kind == 1.0, hit[i], speed[i])) for i in range(3)
    ]


def kernel(
    tile_ref,
    live_ref,
    bvel_ref,
    cells_ref,
    offsets_ref,
    velocity_ref,
    affine_ref,
    stress_ref,
    mass_ref,
    mask_ref,
    friction_ref,
    out_velocity,
    out_affine,
    out_offsets,
    wy_high,
    wy_low,
    patch,
    patch_edge,
    grid,
    edge,
    sums,
    classes,
    planes,
    got_z,
    got_x,
    got_zx,
    got_sums,
    class_z,
    class_x,
    class_zx,
    send_sem,
    recv_sem,
):
    ix, iy, iz = lax.axis_index("gx"), lax.axis_index("gy"), lax.axis_index("gz")
    nx, ny, nz = lax.axis_size("gx"), lax.axis_size("gy"), lax.axis_size("gz")

    def device(dz, dx, dy):
        return {
            "gx": lax.rem(ix + dx + nx, nx),
            "gy": lax.rem(iy + dy + ny, ny),
            "gz": lax.rem(iz + dz + nz, nz),
        }

    barrier = pltpu.get_barrier_semaphore()
    for side in EDGES:
        pl.semaphore_signal(barrier, inc=1, device_id=device(*side), device_id_type=MESH)

    counter = iter(range(2 * len(FACES) + len(EDGES)))

    def sender(src, dst, side):
        slot = next(counter)
        return pltpu.make_async_remote_copy(
            src_ref=src,
            dst_ref=dst,
            send_sem=send_sem.at[slot],
            recv_sem=recv_sem.at[slot],
            device_id=device(*side),
            device_id_type=MESH,
        )

    planes[0] = mask_ref[...].astype(F32)
    planes[1] = friction_ref[...].astype(F32)
    classes[...] = jnp.zeros((2, 128, 128), F32)

    def class_row(z):
        return 64 * (z % 2) + XP * (z // 2)

    for kind in range(2):
        for z in range(4):
            classes[kind, pl.ds(class_row(z + 1) + 1, 16), :] = planes[kind, z]

    zero_patch = jnp.zeros((3, 2, 8, 128), F32)
    zero_lead = jnp.zeros((3, 4, 8, 128), F32)
    for ref in (patch, patch_edge):
        ref[BLOCKS, :, pl.ds(0, 4)] = zero_lead

    def particle(b):
        lanes = pl.ds(pl.multiple_of(b * 128, 128), 128)

        def row(ref, r):
            return jnp.broadcast_to(ref[pl.ds(r, 1), lanes], (8, 128))

        cell = jnp.broadcast_to(cells_ref[pl.ds(b, 1), :], (8, 128))
        frac = [row(offsets_ref, r) for r in range(3)]
        alive = jnp.where(b < live_ref[0], 1.0, 0.0)
        return lanes, row, cell, frac, alive

    def scatter(b):
        lanes, row, cell, frac, alive = particle(b)
        tile = tile_ref[b]
        right = split(along_y(cell, frac[2], (tile & 31) * 4))
        wy_high[b] = right[0]
        wy_low[b] = right[1]
        wz, wz_moment = along_z(cell, frac[0])
        wx, wx_moment = along_x(cell, frac[1])
        mass = jnp.broadcast_to(mass_ref[pl.ds(b, 1), :], (8, 128)) * alive
        push = by_channel([mass] + [mass * row(velocity_ref, i) for i in range(3)])
        zero = jnp.zeros((8, 128), F32)
        scale = 4.0 * DT * alive

        def twist(j):
            return mass * by_channel(
                [zero] + [row(affine_ref, 3 * i + j) for i in range(3)]
            ) - scale * by_channel([zero] + [row(stress_ref, 3 * i + j) for i in range(3)])

        twists = [twist(j) for j in range(3)]
        plain, moment = [], []
        for pair in range(3):
            lead = wz[pair] * push + wz_moment[pair] * twists[0]
            second = wz[pair] * twists[1]
            third = wz[pair] * twists[2]
            for i in range(6):
                plain.append(wx[i] * lead + wx_moment[i] * second)
                moment.append(wx[i] * third)
        left = jnp.concatenate(
            [jnp.concatenate(plain, 0), jnp.concatenate(moment, 0)], 1
        )
        pad = jnp.zeros((112, 256), BF16)
        right = [jnp.concatenate([part, pad], 0) for part in right]
        found = product(left, right, ((1,), (1,)))
        patch[b, :, pl.ds(0, 6)] = found[:, :128].reshape(3, 6, 8, 128)
        patch_edge[b, :, pl.ds(0, 6)] = found[:, 128:].reshape(3, 6, 8, 128)
        patch[b, :, pl.ds(6, 2)] = zero_patch
        patch_edge[b, :, pl.ds(6, 2)] = zero_patch

    def scatter_some(step, carry):
        for u in range(UNROLL):
            scatter(step * UNROLL + u)
        return carry

    lax.fori_loop(0, BLOCKS // UNROLL, scatter_some, 0)

    def collect(source, target):
        def one(q, carry):
            total = jnp.zeros((3, 4, 8, 128), F32)
            for b in range(BLOCKS):
                tx = lax.shift_right_logical(tile_ref[b], 5) & 3
                here, before = tx == q, tx == q - 1
                slot = jnp.where(here | before, b, BLOCKS)
                start = jnp.where(before, 4, 0)
                total = total + source[slot, :, pl.ds(start, 4)]
            target[:, pl.ds(4 * q, 4)] = total
            return carry

        lax.fori_loop(0, 5, one, 0)

    collect(patch_edge, edge)
    edge_rows = edge.reshape(ROWS, 128)
    gap = jnp.zeros((4, 128), F32)
    for c in range(4):
        halves = [edge_rows[pl.ds(2 * c + low, NODES, stride=8), :] for low in range(2)]
        flipped = jnp.concatenate([halves[0], gap, halves[1], gap], 0).T
        sums[pl.ds(4 * c, 4), :] = flipped[:4]
    for kind in range(2):
        flipped = classes[kind].T
        zero = jnp.zeros((1, 128), F32)
        sums[pl.ds(16 + 4 * kind, 4), :] = jnp.concatenate(
            [zero, flipped[0:1], flipped[127:128], zero], 0
        )

    pl.semaphore_wait(barrier, len(EDGES))

    edge_sends = {}
    for index, (dz, dx, dy) in enumerate(EDGES):
        edge_sends[-dz, -dx, -dy] = sender(sums, got_sums.at[index], (dz, dx, dy))
        edge_sends[-dz, -dx, -dy].start()
    received = {(-dz, -dx, -dy): index for index, (dz, dx, dy) in enumerate(EDGES)}

    class_sends = {}
    for dz, dx in FACES:
        zs = {-1: pl.ds(0, 1), 0: pl.ds(0, 4), 1: pl.ds(3, 1)}[dz]
        xs = {-1: pl.ds(0, 8), 0: pl.ds(0, 16), 1: pl.ds(8, 8)}[dx]
        if dx == 0:
            target = class_z.at[(dz + 1) // 2]
        elif dz == 0:
            target = class_x.at[(dx + 1) // 2]
        else:
            target = class_zx.at[dz + 1 + (dx + 1) // 2]
        class_sends[-dz, -dx] = sender(planes.at[:, zs, xs], target, (dz, dx, 0))
        class_sends[-dz, -dx].start()

    collect(patch, grid)
    grid_sends = {}
    for dz, dx in FACES:
        zs = {-1: pl.ds(0, 1), 0: pl.ds(0, 3), 1: pl.ds(2, 1)}[dz]
        xs = {-1: pl.ds(0, 2), 0: pl.ds(0, 18), 1: pl.ds(16, 2)}[dx]
        if dx == 0:
            target = got_z.at[(dz + 1) // 2]
        elif dz == 0:
            target = got_x.at[(dx + 1) // 2]
        else:
            target = got_zx.at[dz + 1 + (dx + 1) // 2]
        grid_sends[-dz, -dx] = sender(grid.at[zs, xs], target, (dz, dx, 0))
        grid_sends[-dz, -dx].start()

    inside = {-1: iz > 0, 0: None, 1: iz < nz - 1}
    bvel = [bvel_ref[i] for i in range(3)]

    lane = lax.broadcasted_iota(jnp.int32, (24, 128), 1)
    column = lax.broadcasted_iota(jnp.int32, (24, 128), 0) & 3
    node = lane & 63
    pair = jnp.where(node >= 2 * XP, 2, jnp.where(node >= XP, 1, 0))
    place = node - XP * pair
    total = sums[...]
    for dz in (-1, 0, 1):
        for dx in (-1, 0, 1):
            part = jnp.zeros((24, 128), F32)
            for dy in (-1, 0, 1):
                if (dz, dx, dy) == (0, 0, 0):
                    continue
                edge_sends[dz, dx, dy].wait_recv()
                came = got_sums[received[dz, dx, dy]]
                if dy == -1:
                    came = jnp.where(column < 2, pltpu.roll(came, 22, 0), 0.0)
                elif dy == 1:
                    came = jnp.where(column >= 2, pltpu.roll(came, 2, 0), 0.0)
                part = part + came
            shift = (16 * dx + 2 * XP * dz) % 128
            if shift:
                part = pltpu.roll(part, shift, 1)
            keep = node < NODES
            if dx == -1:
                keep = keep & (place < 2)
            elif dx == 1:
                keep = keep & (place >= 16) & (place < 18)
            if dz == -1:
                keep = keep & (pair == 0) & inside[-1]
            elif dz == 1:
                keep = keep & (pair == 2) & inside[1]
            total = total + jnp.where(keep, part, 0.0)
    new = contact(
        total[0:4],
        [total[4:8], total[8:12], total[12:16]],
        total[16:20],
        total[20:24],
        bvel,
    )
    depth = 2 * pair[:4] + lax.shift_right_logical(lane[:4], 6)
    outside = ((depth == 0) & (iz == 0)) | ((depth == 5) & (iz == nz - 1))
    tail = jnp.zeros((124, 128), F32)
    for i in range(3):
        rows = jnp.concatenate([jnp.where(outside, 0.0, new[i]), tail], 0).T
        for low in range(2):
            edge_rows[pl.ds(2 * i + 2 + low, NODES, stride=8), :] = rows[64 * low : 64 * low + NODES]

    for dz, dx in FACES:
        class_sends[dz, dx].wait_recv()
    for kind in range(2):
        for side, row, x in ((0, 7, 0), (1, 0, 17)):
            for z in range(4):
                classes[kind, pl.ds(class_row(z + 1) + x, 1), :] = class_x[
                    1 - side, kind, z, pl.ds(row, 1), :
                ]
        for side, z in ((0, 0), (1, 5)):
            classes[kind, pl.ds(class_row(z) + 1, 16), :] = class_z[1 - side, kind, 0]
            for other, row, x in ((0, 7, 0), (1, 0, 17)):
                classes[kind, pl.ds(class_row(z) + x, 1), :] = class_zx[
                    2 * (1 - side) + (1 - other), kind, 0, pl.ds(row, 1), :
                ]

    for dz, dx in FACES:
        grid_sends[dz, dx].wait_recv()
        grid_sends[-dz, -dx].wait_send()
    for dz, dx in FACES:
        zs = {-1: pl.ds(0, 1), 0: pl.ds(0, 3), 1: pl.ds(2, 1)}[dz]
        xs = {-1: pl.ds(0, 2), 0: pl.ds(0, 18), 1: pl.ds(16, 2)}[dx]
        if dx == 0:
            came = got_z[(1 - dz) // 2]
        elif dz == 0:
            came = got_x[(1 - dx) // 2]
        else:
            came = got_zx[1 - dz + (1 - dx) // 2]
        if dz:
            came = jnp.where(inside[dz], came, 0.0)
        grid[zs, xs] = grid[zs, xs] + came
    grid_rows = grid.reshape(ROWS, 128)
    number = lax.broadcasted_iota(jnp.int32, (NODES, 128), 0)
    for low in range(2):
        load = [grid_rows[pl.ds(2 * c + low, NODES, stride=8), :] for c in range(4)]
        new = contact(
            load[0],
            load[1:],
            classes[0, pl.ds(64 * low, NODES), :],
            classes[1, pl.ds(64 * low, NODES), :],
            bvel,
        )
        if low == 0:
            outside = (number < XP) & (iz == 0)
        else:
            outside = (number >= 2 * XP) & (iz == nz - 1)
        for i in range(3):
            grid_rows[pl.ds(2 * i + 2 + low, NODES, stride=8), :] = jnp.where(
                outside, 0.0, new[i]
            )

    def gather(b):
        lanes, row, cell, frac, alive = particle(b)
        first = (lax.shift_right_logical(tile_ref[b], 5) & 3) * 4
        left = jnp.concatenate(
            [ref[:, pl.ds(first, 6)].reshape(144, 128) for ref in (grid, edge)], 1
        )
        pad = jnp.zeros((112, 256), BF16)
        right = [jnp.concatenate([ref[b], pad], 0) for ref in (wy_high, wy_low)]
        found = product(left, right, ((1,), (0,)))
        plain = found[:, :128].reshape(3, 6, 8, 128)
        moment = found[:, 128:].reshape(3, 6, 8, 128)
        wz, wz_moment = along_z(cell, frac[0])
        wx, wx_moment = along_x(cell, frac[1])
        totals = [jnp.zeros((8, 128), F32) for _ in range(4)]
        for pair in range(3):
            sum_w = sum(wx[i] * plain[pair, i] for i in range(6))
            sum_x = sum(wx_moment[i] * plain[pair, i] for i in range(6))
            sum_y = sum(wx[i] * moment[pair, i] for i in range(6))
            totals[0] = totals[0] + wz[pair] * sum_w
            totals[1] = totals[1] + wz_moment[pair] * sum_w
            totals[2] = totals[2] + wz[pair] * sum_x
            totals[3] = totals[3] + wz[pair] * sum_y
        totals = [(t + pltpu.roll(t, 7, 0)) * alive for t in totals]
        for i in range(3):
            at = 2 * i + 2
            moved = totals[0][at : at + 1]
            out_velocity[pl.ds(i, 1), lanes] = moved
            out_offsets[pl.ds(i, 1), lanes] = frac[i][:1] * alive + DT * moved
            for j in range(3):
                out_affine[pl.ds(3 * i + j, 1), lanes] = 4.0 * totals[j + 1][at : at + 1]

    def gather_some(step, carry):
        for u in range(UNROLL):
            gather(step * UNROLL + u)
        return carry

    lax.fori_loop(0, BLOCKS // UNROLL, gather_some, 0)
    for send in list(edge_sends.values()) + list(class_sends.values()):
        send.wait_send()


def on_device(
    cells,
    offsets,
    velocity,
    affine,
    stress,
    mass,
    block_tile,
    live_blocks,
    bucket_mask,
    friction_class,
    bucket_velocity,
):
    smem = pl.BlockSpec(memory_space=pltpu.SMEM)
    vmem = pl.BlockSpec(memory_space=pltpu.VMEM)
    count = cells.shape[0]
    copies = 2 * len(FACES) + len(EDGES)
    return pl.pallas_call(
        kernel,
        out_shape=(
            jax.ShapeDtypeStruct((3, count), F32),
            jax.ShapeDtypeStruct((9, count), F32),
            jax.ShapeDtypeStruct((3, count), F32),
        ),
        in_specs=[smem] * 3 + [vmem] * 8,
        out_specs=(vmem,) * 3,
        scratch_shapes=[
            pltpu.VMEM((BLOCKS, 144, 256), BF16),
            pltpu.VMEM((BLOCKS, 144, 256), BF16),
            pltpu.VMEM((BLOCKS + 1, 3, 8, 8, 128), F32),
            pltpu.VMEM((BLOCKS + 1, 3, 8, 8, 128), F32),
            pltpu.VMEM((3, XP, 8, 128), F32),
            pltpu.VMEM((3, XP, 8, 128), F32),
            pltpu.VMEM((24, 128), F32),
            pltpu.VMEM((2, 128, 128), F32),
            pltpu.VMEM((2, 4, 16, 128), F32),
            pltpu.VMEM((2, 1, 18, 8, 128), F32),
            pltpu.VMEM((2, 3, 2, 8, 128), F32),
            pltpu.VMEM((4, 1, 2, 8, 128), F32),
            pltpu.VMEM((len(EDGES), 24, 128), F32),
            pltpu.VMEM((2, 2, 1, 16, 128), F32),
            pltpu.VMEM((2, 2, 4, 8, 128), F32),
            pltpu.VMEM((4, 2, 1, 8, 128), F32),
            pltpu.SemaphoreType.DMA((copies,)),
            pltpu.SemaphoreType.DMA((copies,)),
        ],
        compiler_params=pltpu.CompilerParams(
            collective_id=0, has_side_effects=True, vmem_limit_bytes=40 * 1024 * 1024
        ),
    )(
        block_tile,
        live_blocks,
        bucket_velocity,
        cells.reshape(BLOCKS, 128),
        offsets,
        velocity,
        affine,
        stress,
        mass.reshape(BLOCKS, 128),
        bucket_mask,
        friction_class,
    )


def solution(mesh):
    along = ("gx", "gy", "gz")
    return jax.shard_map(
        on_device,
        mesh=mesh,
        in_specs=(
            P(along),
            P(None, along),
            P(None, along),
            P(None, along),
            P(None, along),
            P(along),
            P(along),
            P(along),
            P("gz", "gx", "gy"),
            P("gz", "gx", "gy"),
            P(),
        ),
        out_specs=(P(None, along), P(None, along), P(None, along)),
        check_vma=False,
    )
```

time: 109 us -> 34.4 us (0.32)
  the two profiles are of different devices: /device:TPU:71 before, /device:TPU:1 now
where the time goes in v1:
time: 34.4 us; the launch traced here: 33.9 us
  Pallas kernels  23.8 us (69%)
  local copies, waits for them, and re-layouts  8.77 us (25%)
  between operations  1.31 us (4%)
    pallas_call x1, Pallas kernels, on_device(): pl.pallas_call(kernel, out_shape=(jax.ShapeDtypeStruct((3, count), F32),...  23.8 us
    unnamed x23, local copies, waits for them, and re-layouts  8.77 us

profile of v1, /device:TPU:1, one launch (start us, length us, event | category | flops | bytes accessed | tf_op | source)
XLA Modules:
  0.0 33.9 jit_solution(13851217362596356878)
XLA Ops:
  1.3 0.0 copy-start.8
  1.3 0.0 copy-start.9
  1.3 0.6 %copy-done.8 = s32[16]{0:T(128)S(1)} copy-done((s32[16]{0:T(128)S(1)}, s32[16]{0:T(128)}, u32[]{:S(2)}) %copy-start.8) | copy-done | bytes 88
  1.9 0.0 copy-done.9
  2.0 0.0 copy-start
  2.0 0.9 %copy-done = f32[9,2048]{1,0:T(8,128)S(1)} copy-done((f32[9,2048]{1,0:T(8,128)S(1)}, f32[9,2048]{1,0:T(8,128)}, u32[]{:S(2)}) %copy-start) | copy-done | bytes 73752
  2.9 0.0 copy-start.1
  2.9 0.9 %copy-done.1 = f32[9,2048]{1,0:T(8,128)S(1)} copy-done((f32[9,2048]{1,0:T(8,128)S(1)}, f32[9,2048]{1,0:T(8,128)}, u32[]{:S(2)}) %copy-start.1) | copy-done | bytes 73752
  3.8 0.0 copy-start.2
  3.8 0.8 %copy-done.2 = f32[3,2048]{1,0:T(4,128)S(1)} copy-done((f32[3,2048]{1,0:T(4,128)S(1)}, f32[3,2048]{1,0:T(4,128)}, u32[]{:S(2)}) %copy-start.2) | copy-done | bytes 24600
  4.5 0.0 copy-start.3
  4.5 0.8 %copy-done.3 = f32[3,2048]{1,0:T(4,128)S(1)} copy-done((f32[3,2048]{1,0:T(4,128)S(1)}, f32[3,2048]{1,0:T(4,128)}, u32[]{:S(2)}) %copy-start.3) | copy-done | bytes 24600
  5.3 0.0 copy-start.4
  5.3 0.8 %copy-done.4 = s32[4,16,128]{2,1,0:T(8,128)S(1)} copy-done((s32[4,16,128]{2,1,0:T(8,128)S(1)}, s32[4,16,128]{2,1,0:T(8,128)}, u32[]{:S(2)}) %copy-start.4) | copy-done | bytes 32792
  6.0 0.0 copy-start.5
  6.0 0.8 %copy-done.5 = s32[4,16,128]{2,1,0:T(8,128)S(1)} copy-done((s32[4,16,128]{2,1,0:T(8,128)S(1)}, s32[4,16,128]{2,1,0:T(8,128)}, u32[]{:S(2)}) %copy-start.5) | copy-done | bytes 32792
  6.8 0.0 copy-start.6
  6.8 0.7 %copy-done.6 = s32[2048]{0:T(1024)S(1)} copy-done((s32[2048]{0:T(1024)S(1)}, s32[2048]{0:T(1024)}, u32[]{:S(2)}) %copy-start.6) | copy-done | bytes 8216
  7.5 0.0 copy-start.7
  7.5 0.7 %copy-done.7 = f32[2048]{0:T(1024)S(1)} copy-done((f32[2048]{0:T(1024)S(1)}, f32[2048]{0:T(1024)}, u32[]{:S(2)}) %copy-start.7) | copy-done | bytes 8216
  8.2 23.8 %shard_map.130 = (f32[3,2048]{1,0:T(4,128)S(1)}, f32[9,2048]{1,0:T(8,128)S(1)}, f32[3,2048]{1,0:T(4,128)S(1)}) custom-call(s32[16]{0:T(128)S(1)} %copy-done.8, s32[1]{0:T(128)S(6)} %copy.17.live_ref, f32[3]{0:T(128)S(1)} %copy-done.9, s32[16,128]{1,0:T(8,128)S(1)} %bitcast.2, f32[3,2048]{1,0:T(4,128)S(1)} %copy-done.2, f32[3,2048]{1,0:T(4,128)S(1)} %copy-done.3, ...), custom_call_target="tpu_custom_call" | custom-call | tf_op jit(solution)/shard_map/pallas_call | solution.py:496
  32.0 0.6 %copy.18 = f32[3,2048]{1,0:T(4,128)} copy(f32[3,2048]{1,0:T(4,128)S(1)} %get-tuple-element.6) | data formatting | bytes 49152
  32.6 0.7 %copy.19 = f32[9,2048]{1,0:T(8,128)} copy(f32[9,2048]{1,0:T(8,128)S(1)} %get-tuple-element.7) | data formatting | bytes 147456
  33.2 0.6 %copy.20 = f32[3,2048]{1,0:T(4,128)} copy(f32[3,2048]{1,0:T(4,128)S(1)} %get-tuple-element.8) | data formatting | bytes 49152
Async XLA Ops:
  1.3 0.7 %copy-start.8 = (s32[16]{0:T(128)S(1)}, s32[16]{0:T(128)}, u32[]{:S(2)}) copy-start(s32[16]{0:T(128)} %tile_ref.1) | copy-start | bytes 196
  1.3 0.7 %copy-start.9 = (f32[3]{0:T(128)S(1)}, f32[3]{0:T(128)}, u32[]{:S(2)}) copy-start(f32[3]{0:T(128)} %bvel_ref.1) | copy-start | bytes 40
  2.0 0.9 %copy-start = (f32[9,2048]{1,0:T(8,128)S(1)}, f32[9,2048]{1,0:T(8,128)}, u32[]{:S(2)}) copy-start(f32[9,2048]{1,0:T(8,128)} %affine_ref.1) | copy-start | bytes 221188
  2.9 0.9 %copy-start.1 = (f32[9,2048]{1,0:T(8,128)S(1)}, f32[9,2048]{1,0:T(8,128)}, u32[]{:S(2)}) copy-start(f32[9,2048]{1,0:T(8,128)} %stress_ref.1) | copy-start | bytes 221188
  3.8 0.8 %copy-start.2 = (f32[3,2048]{1,0:T(4,128)S(1)}, f32[3,2048]{1,0:T(4,128)}, u32[]{:S(2)}) copy-start(f32[3,2048]{1,0:T(4,128)} %offsets_ref.1) | copy-start | bytes 73732
  4.5 0.8 %copy-start.3 = (f32[3,2048]{1,0:T(4,128)S(1)}, f32[3,2048]{1,0:T(4,128)}, u32[]{:S(2)}) copy-start(f32[3,2048]{1,0:T(4,128)} %velocity_ref.1) | copy-start | bytes 73732
  5.3 0.8 %copy-start.4 = (s32[4,16,128]{2,1,0:T(8,128)S(1)}, s32[4,16,128]{2,1,0:T(8,128)}, u32[]{:S(2)}) copy-start(s32[4,16,128]{2,1,0:T(8,128)} %mask_ref.1) | copy-start | bytes 98308
  6.0 0.8 %copy-start.5 = (s32[4,16,128]{2,1,0:T(8,128)S(1)}, s32[4,16,128]{2,1,0:T(8,128)}, u32[]{:S(2)}) copy-start(s32[4,16,128]{2,1,0:T(8,128)} %friction_ref.1) | copy-start | bytes 98308
  6.8 0.7 %copy-start.6 = (s32[2048]{0:T(1024)S(1)}, s32[2048]{0:T(1024)}, u32[]{:S(2)}) copy-start(s32[2048]{0:T(1024)} %param.11) | copy-start | bytes 24580
  7.5 0.7 %copy-start.7 = (f32[2048]{0:T(1024)S(1)}, f32[2048]{0:T(1024)}, u32[]{:S(2)}) copy-start(f32[2048]{0:T(1024)} %param.16) | copy-start | bytes 24580

commit v2 on v1

--- a/solution.py
+++ b/solution.py
@@ -14,7 +14,9 @@
 FRICTION = (0.1, 0.4, 0.8, 1.2)
 
 BLOCKS = 16
-UNROLL = 2
+UNROLL = 8
+VMEM_SPREAD = 52 * 1024 * 1024
+VMEM_COLLECT = 16 * 1024 * 1024
 XP = 20
 ROWS = 3 * XP * 8
 NODES = 3 * XP
@@ -23,13 +25,10 @@
 MESH = pl.DeviceIdType.MESH
 
 FACES = [(dz, dx) for dz in (-1, 0, 1) for dx in (-1, 0, 1) if (dz, dx) != (0, 0)]
-EDGES = [
-    (dz, dx, dy)
-    for dz in (-1, 0, 1)
-    for dx in (-1, 0, 1)
-    for dy in (-1, 0, 1)
-    if (dz, dx, dy) != (0, 0, 0)
-]
+SLOT = {side: index for index, side in enumerate(FACES)}
+SENDS = 3 * len(FACES) + 4
+Z_PLANE = {-1: 0, 1: 3}
+Z_PAIR = {-1: 0, 1: 2}
 
 
 def spline(frac):
@@ -139,42 +138,89 @@
     ]
 
 
-def kernel(
+def particle(b, tile_ref, live_ref, cells_ref, offsets_ref):
+    lanes = pl.ds(pl.multiple_of(b * 128, 128), 128)
+
+    def row(ref, r):
+        return jnp.broadcast_to(ref[pl.ds(r, 1), lanes], (8, 128))
+
+    cell = jnp.broadcast_to(cells_ref[pl.ds(b, 1), :], (8, 128))
+    frac = [row(offsets_ref, r) for r in range(3)]
+    alive = jnp.where(b < live_ref[0], 1.0, 0.0)
+    return lanes, row, cell, frac, alive
+
+
+def spread(
+    tile_hbm,
+    live_hbm,
+    bvel_hbm,
+    cells_hbm,
+    offsets_hbm,
+    velocity_hbm,
+    affine_hbm,
+    stress_hbm,
+    mass_hbm,
+    mask_hbm,
+    friction_hbm,
     tile_ref,
     live_ref,
-    bvel_ref,
     cells_ref,
     offsets_ref,
+    wy_high,
+    wy_low,
+    grid,
+    edge,
+    bvel_ref,
     velocity_ref,
     affine_ref,
     stress_ref,
     mass_ref,
     mask_ref,
     friction_ref,
-    out_velocity,
-    out_affine,
-    out_offsets,
-    wy_high,
-    wy_low,
     patch,
     patch_edge,
-    grid,
-    edge,
     sums,
+    folded,
     classes,
     planes,
+    sides,
+    ends,
     got_z,
     got_x,
     got_zx,
-    got_sums,
+    got_y,
+    got_folded,
     class_z,
     class_x,
-    class_zx,
+    class_y,
+    load_sem,
     send_sem,
     recv_sem,
 ):
+    loads = [
+        pltpu.make_async_copy(source, target, load_sem.at[index])
+        for index, (source, target) in enumerate(
+            (
+                (cells_hbm, cells_ref),
+                (offsets_hbm, offsets_ref),
+                (tile_hbm, tile_ref),
+                (live_hbm, live_ref),
+                (mass_hbm, mass_ref),
+                (velocity_hbm, velocity_ref),
+                (affine_hbm, affine_ref),
+                (stress_hbm, stress_ref),
+                (mask_hbm, mask_ref),
+                (friction_hbm, friction_ref),
+                (bvel_hbm, bvel_ref),
+            )
+        )
+    ]
+    for load in loads:
+        load.start()
+
     ix, iy, iz = lax.axis_index("gx"), lax.axis_index("gy"), lax.axis_index("gz")
     nx, ny, nz = lax.axis_size("gx"), lax.axis_size("gy"), lax.axis_size("gz")
+    above, below = iz < nz - 1, iz > 0
 
     def device(dz, dx, dy):
         return {
@@ -183,52 +229,83 @@
             "gz": lax.rem(iz + dz + nz, nz),
         }
 
+    def where_z(dz, action):
+        if dz == 0:
+            action()
+        else:
+            pl.when(above if dz == 1 else below)(action)
+
     barrier = pltpu.get_barrier_semaphore()
-    for side in EDGES:
-        pl.semaphore_signal(barrier, inc=1, device_id=device(*side), device_id_type=MESH)
-
-    counter = iter(range(2 * len(FACES) + len(EDGES)))
-
-    def sender(src, dst, side):
+
+    def greet(dz, dx, dy):
+        where_z(
+            dz,
+            lambda: pl.semaphore_signal(
+                barrier, inc=1, device_id=device(dz, dx, dy), device_id_type=MESH
+            ),
+        )
+
+    for dz, dx in FACES:
+        greet(dz, dx, 0)
+    for dy in (-1, 1):
+        greet(0, 0, dy)
+
+    counter = iter(range(SENDS))
+
+    def sender(src, dst, dz, dx, dy):
         slot = next(counter)
         return pltpu.make_async_remote_copy(
             src_ref=src,
             dst_ref=dst,
             send_sem=send_sem.at[slot],
             recv_sem=recv_sem.at[slot],
-            device_id=device(*side),
+            device_id=device(dz, dx, dy),
             device_id_type=MESH,
         )
 
-    planes[0] = mask_ref[...].astype(F32)
-    planes[1] = friction_ref[...].astype(F32)
+    class_sends, grid_sends, edge_sends = {}, {}, {}
+    for dz, dx in FACES:
+        came = (-dz, -dx)
+        if dx == 0:
+            class_sends[came] = sender(
+                planes.at[:, Z_PLANE[dz]], class_z.at[(1 + dz) // 2], dz, dx, 0
+            )
+        else:
+            class_sends[came] = sender(
+                sides.at[(1 + dx) // 2], class_x.at[SLOT[dz, dx]], dz, dx, 0
+            )
+        if dx == 0:
+            grid_sends[came] = sender(
+                grid.at[Z_PAIR[dz], pl.ds(0, 18)], got_z.at[(1 + dz) // 2], dz, dx, 0
+            )
+        elif dz == 0:
+            grid_sends[came] = sender(
+                grid.at[:, pl.ds(8 + 8 * dx, 2)], got_x.at[(1 + dx) // 2], dz, dx, 0
+            )
+        else:
+            grid_sends[came] = sender(
+                grid.at[Z_PAIR[dz], pl.ds(8 + 8 * dx, 2)], got_zx.at[SLOT[dz, dx]], dz, dx, 0
+            )
+        edge_sends[came] = sender(folded, got_folded.at[SLOT[dz, dx]], dz, dx, 0)
+    sum_y = {-dy: sender(sums.at[(1 + dy) // 2], got_y.at[(1 + dy) // 2], 0, 0, dy) for dy in (-1, 1)}
+    class_ends = {-dy: sender(ends, class_y.at[(1 + dy) // 2], 0, 0, dy) for dy in (-1, 1)}
+
+    def slot_from(dz, dx):
+        return SLOT[-dz, -dx]
+
     classes[...] = jnp.zeros((2, 128, 128), F32)
+    ends[...] = jnp.zeros((8, 128), F32)
 
     def class_row(z):
         return 64 * (z % 2) + XP * (z // 2)
-
-    for kind in range(2):
-        for z in range(4):
-            classes[kind, pl.ds(class_row(z + 1) + 1, 16), :] = planes[kind, z]
 
     zero_patch = jnp.zeros((3, 2, 8, 128), F32)
     zero_lead = jnp.zeros((3, 4, 8, 128), F32)
     for ref in (patch, patch_edge):
         ref[BLOCKS, :, pl.ds(0, 4)] = zero_lead
 
-    def particle(b):
-        lanes = pl.ds(pl.multiple_of(b * 128, 128), 128)
-
-        def row(ref, r):
-            return jnp.broadcast_to(ref[pl.ds(r, 1), lanes], (8, 128))
-
-        cell = jnp.broadcast_to(cells_ref[pl.ds(b, 1), :], (8, 128))
-        frac = [row(offsets_ref, r) for r in range(3)]
-        alive = jnp.where(b < live_ref[0], 1.0, 0.0)
-        return lanes, row, cell, frac, alive
-
     def scatter(b):
-        lanes, row, cell, frac, alive = particle(b)
+        lanes, row, cell, frac, alive = particle(b, tile_ref, live_ref, cells_ref, offsets_ref)
         tile = tile_ref[b]
         right = split(along_y(cell, frac[2], (tile & 31) * 4))
         wy_high[b] = right[0]
@@ -265,7 +342,29 @@
         patch[b, :, pl.ds(6, 2)] = zero_patch
         patch_edge[b, :, pl.ds(6, 2)] = zero_patch
 
+    def send_classes():
+        loads[8].wait()
+        loads[9].wait()
+        planes[0] = mask_ref[...].astype(F32)
+        planes[1] = friction_ref[...].astype(F32)
+        flat = planes.reshape(128, 128)
+        sides[0] = flat[pl.ds(0, 8, stride=16), :]
+        sides[1] = flat[pl.ds(15, 8, stride=16), :]
+        for kind in range(2):
+            for z in range(4):
+                classes[kind, pl.ds(class_row(z + 1) + 1, 16), :] = planes[kind, z]
+        partners = len(FACES) + 2
+        pl.semaphore_wait(
+            barrier, partners - 3 * (1 - above.astype(jnp.int32)) - 3 * (1 - below.astype(jnp.int32))
+        )
+        for dz, dx in FACES:
+            where_z(dz, class_sends[-dz, -dx].start)
+
+    for load in loads[:8]:
+        load.wait()
+
     def scatter_some(step, carry):
+        pl.when(step == 1)(send_classes)
         for u in range(UNROLL):
             scatter(step * UNROLL + u)
         return carry
@@ -292,129 +391,73 @@
     for c in range(4):
         halves = [edge_rows[pl.ds(2 * c + low, NODES, stride=8), :] for low in range(2)]
         flipped = jnp.concatenate([halves[0], gap, halves[1], gap], 0).T
-        sums[pl.ds(4 * c, 4), :] = flipped[:4]
+        sums[0, pl.ds(2 * c, 2), :] = flipped[0:2]
+        sums[1, pl.ds(2 * c, 2), :] = flipped[2:4]
+    for dy in (-1, 1):
+        sum_y[-dy].start()
+
+    collect(patch, grid)
+    for dz, dx in FACES:
+        where_z(dz, grid_sends[-dz, -dx].start)
+
+    for dy in (-1, 1):
+        sum_y[dy].wait_recv()
+    folded[0] = sums[0] + got_y[1]
+    folded[1] = sums[1] + got_y[0]
+    for dz, dx in FACES:
+        where_z(dz, edge_sends[-dz, -dx].start)
+
+    for dz, dx in FACES:
+
+        def take(dz=dz, dx=dx):
+            class_sends[dz, dx].wait_recv()
+            if dx == 0:
+                z = 0 if dz == -1 else 5
+                for kind in range(2):
+                    classes[kind, pl.ds(class_row(z) + 1, 16), :] = class_z[(1 - dz) // 2, kind]
+            else:
+                x = 0 if dx == -1 else 17
+                for kind in range(2):
+                    for z in range(4) if dz == 0 else (Z_PLANE[-dz],):
+                        classes[kind, pl.ds(class_row(z + 1 + 4 * dz) + x, 1), :] = class_x[
+                            slot_from(dz, dx), pl.ds(4 * kind + z, 1), :
+                        ]
+
+        where_z(dz, take)
     for kind in range(2):
         flipped = classes[kind].T
-        zero = jnp.zeros((1, 128), F32)
-        sums[pl.ds(16 + 4 * kind, 4), :] = jnp.concatenate(
-            [zero, flipped[0:1], flipped[127:128], zero], 0
-        )
-
-    pl.semaphore_wait(barrier, len(EDGES))
-
-    edge_sends = {}
-    for index, (dz, dx, dy) in enumerate(EDGES):
-        edge_sends[-dz, -dx, -dy] = sender(sums, got_sums.at[index], (dz, dx, dy))
-        edge_sends[-dz, -dx, -dy].start()
-    received = {(-dz, -dx, -dy): index for index, (dz, dx, dy) in enumerate(EDGES)}
-
-    class_sends = {}
-    for dz, dx in FACES:
-        zs = {-1: pl.ds(0, 1), 0: pl.ds(0, 4), 1: pl.ds(3, 1)}[dz]
-        xs = {-1: pl.ds(0, 8), 0: pl.ds(0, 16), 1: pl.ds(8, 8)}[dx]
-        if dx == 0:
-            target = class_z.at[(dz + 1) // 2]
-        elif dz == 0:
-            target = class_x.at[(dx + 1) // 2]
-        else:
-            target = class_zx.at[dz + 1 + (dx + 1) // 2]
-        class_sends[-dz, -dx] = sender(planes.at[:, zs, xs], target, (dz, dx, 0))
-        class_sends[-dz, -dx].start()
-
-    collect(patch, grid)
-    grid_sends = {}
-    for dz, dx in FACES:
-        zs = {-1: pl.ds(0, 1), 0: pl.ds(0, 3), 1: pl.ds(2, 1)}[dz]
-        xs = {-1: pl.ds(0, 2), 0: pl.ds(0, 18), 1: pl.ds(16, 2)}[dx]
-        if dx == 0:
-            target = got_z.at[(dz + 1) // 2]
-        elif dz == 0:
-            target = got_x.at[(dx + 1) // 2]
-        else:
-            target = got_zx.at[dz + 1 + (dx + 1) // 2]
-        grid_sends[-dz, -dx] = sender(grid.at[zs, xs], target, (dz, dx, 0))
-        grid_sends[-dz, -dx].start()
-
-    inside = {-1: iz > 0, 0: None, 1: iz < nz - 1}
-    bvel = [bvel_ref[i] for i in range(3)]
-
-    lane = lax.broadcasted_iota(jnp.int32, (24, 128), 1)
-    column = lax.broadcasted_iota(jnp.int32, (24, 128), 0) & 3
-    node = lane & 63
-    pair = jnp.where(node >= 2 * XP, 2, jnp.where(node >= XP, 1, 0))
-    place = node - XP * pair
-    total = sums[...]
-    for dz in (-1, 0, 1):
-        for dx in (-1, 0, 1):
-            part = jnp.zeros((24, 128), F32)
-            for dy in (-1, 0, 1):
-                if (dz, dx, dy) == (0, 0, 0):
-                    continue
-                edge_sends[dz, dx, dy].wait_recv()
-                came = got_sums[received[dz, dx, dy]]
-                if dy == -1:
-                    came = jnp.where(column < 2, pltpu.roll(came, 22, 0), 0.0)
-                elif dy == 1:
-                    came = jnp.where(column >= 2, pltpu.roll(came, 2, 0), 0.0)
-                part = part + came
-            shift = (16 * dx + 2 * XP * dz) % 128
-            if shift:
-                part = pltpu.roll(part, shift, 1)
-            keep = node < NODES
-            if dx == -1:
-                keep = keep & (place < 2)
-            elif dx == 1:
-                keep = keep & (place >= 16) & (place < 18)
-            if dz == -1:
-                keep = keep & (pair == 0) & inside[-1]
-            elif dz == 1:
-                keep = keep & (pair == 2) & inside[1]
-            total = total + jnp.where(keep, part, 0.0)
-    new = contact(
-        total[0:4],
-        [total[4:8], total[8:12], total[12:16]],
-        total[16:20],
-        total[20:24],
-        bvel,
-    )
-    depth = 2 * pair[:4] + lax.shift_right_logical(lane[:4], 6)
-    outside = ((depth == 0) & (iz == 0)) | ((depth == 5) & (iz == nz - 1))
-    tail = jnp.zeros((124, 128), F32)
+        ends[pl.ds(2 * kind, 1), :] = flipped[0:1]
+        ends[pl.ds(2 * kind + 1, 1), :] = flipped[127:128]
+    for dy in (-1, 1):
+        class_ends[-dy].start()
+
+    bvel = []
+    loads[10].wait()
     for i in range(3):
-        rows = jnp.concatenate([jnp.where(outside, 0.0, new[i]), tail], 0).T
-        for low in range(2):
-            edge_rows[pl.ds(2 * i + 2 + low, NODES, stride=8), :] = rows[64 * low : 64 * low + NODES]
-
-    for dz, dx in FACES:
-        class_sends[dz, dx].wait_recv()
-    for kind in range(2):
-        for side, row, x in ((0, 7, 0), (1, 0, 17)):
-            for z in range(4):
-                classes[kind, pl.ds(class_row(z + 1) + x, 1), :] = class_x[
-                    1 - side, kind, z, pl.ds(row, 1), :
-                ]
-        for side, z in ((0, 0), (1, 5)):
-            classes[kind, pl.ds(class_row(z) + 1, 16), :] = class_z[1 - side, kind, 0]
-            for other, row, x in ((0, 7, 0), (1, 0, 17)):
-                classes[kind, pl.ds(class_row(z) + x, 1), :] = class_zx[
-                    2 * (1 - side) + (1 - other), kind, 0, pl.ds(row, 1), :
-                ]
-
-    for dz, dx in FACES:
-        grid_sends[dz, dx].wait_recv()
-        grid_sends[-dz, -dx].wait_send()
-    for dz, dx in FACES:
-        zs = {-1: pl.ds(0, 1), 0: pl.ds(0, 3), 1: pl.ds(2, 1)}[dz]
-        xs = {-1: pl.ds(0, 2), 0: pl.ds(0, 18), 1: pl.ds(16, 2)}[dx]
-        if dx == 0:
-            came = got_z[(1 - dz) // 2]
-        elif dz == 0:
-            came = got_x[(1 - dx) // 2]
-        else:
-            came = got_zx[1 - dz + (1 - dx) // 2]
-        if dz:
-            came = jnp.where(inside[dz], came, 0.0)
-        grid[zs, xs] = grid[zs, xs] + came
+        bvel.append(bvel_ref[i])
+
+    for dz, dx in FACES:
+
+        def add(dz=dz, dx=dx):
+            grid_sends[dz, dx].wait_recv()
+
+        where_z(dz, add)
+    for dz, dx in FACES:
+        where_z(dz, grid_sends[-dz, -dx].wait_send)
+    for dz, dx in FACES:
+
+        def add(dz=dz, dx=dx):
+            if dx == 0:
+                pair = Z_PAIR[dz]
+                grid[pair, pl.ds(0, 18)] = grid[pair, pl.ds(0, 18)] + got_z[(1 - dz) // 2]
+            elif dz == 0:
+                xs = pl.ds(8 + 8 * dx, 2)
+                grid[:, xs] = grid[:, xs] + got_x[(1 - dx) // 2]
+            else:
+                pair, xs = Z_PAIR[dz], pl.ds(8 + 8 * dx, 2)
+                grid[pair, xs] = grid[pair, xs] + got_zx[slot_from(dz, dx)]
+
+        where_z(dz, add)
     grid_rows = grid.reshape(ROWS, 128)
     number = lax.broadcasted_iota(jnp.int32, (NODES, 128), 0)
     for low in range(2):
@@ -435,8 +478,74 @@
                 outside, 0.0, new[i]
             )
 
+    lane = lax.broadcasted_iota(jnp.int32, (8, 128), 1)
+    node = lane & 63
+    pair = jnp.where(node >= 2 * XP, 2, jnp.where(node >= XP, 1, 0))
+    place = node - XP * pair
+    totals = [folded[0], folded[1]]
+    for dz, dx in FACES:
+        where_z(dz, edge_sends[dz, dx].wait_recv)
+        keep = node < NODES
+        if dx == -1:
+            keep = keep & (place < 2)
+        elif dx == 1:
+            keep = keep & (place >= 16) & (place < 18)
+        if dz == -1:
+            keep = keep & (pair == 0) & below
+        elif dz == 1:
+            keep = keep & (pair == 2) & above
+        shift = (16 * dx + 2 * XP * dz) % 128
+        for side in range(2):
+            came = pltpu.roll(got_folded[slot_from(dz, dx), side], shift, 1)
+            totals[side] = totals[side] + jnp.where(keep, came, 0.0)
+    for dy in (-1, 1):
+        class_ends[dy].wait_recv()
+    kinds = []
+    for kind in range(2):
+        low, high = pl.ds(2 * kind, 1), pl.ds(2 * kind + 1, 1)
+        kinds.append(
+            jnp.concatenate([class_y[1, high, :], ends[low, :], ends[high, :], class_y[0, low, :]], 0)
+        )
+    parts = [
+        jnp.concatenate([totals[0][2 * c : 2 * c + 2], totals[1][2 * c : 2 * c + 2]], 0)
+        for c in range(4)
+    ]
+    new = contact(parts[0], parts[1:], kinds[0], kinds[1], bvel)
+    depth = 2 * pair[:4] + lax.shift_right_logical(lane[:4], 6)
+    outside = ((depth == 0) & (iz == 0)) | ((depth == 5) & (iz == nz - 1))
+    tail = jnp.zeros((124, 128), F32)
+    for i in range(3):
+        rows = jnp.concatenate([jnp.where(outside, 0.0, new[i]), tail], 0).T
+        for low in range(2):
+            edge_rows[pl.ds(2 * i + 2 + low, NODES, stride=8), :] = rows[64 * low : 64 * low + NODES]
+
+    for dz, dx in FACES:
+
+        def finish(came=(-dz, -dx)):
+            class_sends[came].wait_send()
+            edge_sends[came].wait_send()
+
+        where_z(dz, finish)
+    for dy in (-1, 1):
+        sum_y[dy].wait_send()
+        class_ends[dy].wait_send()
+
+
+def collect_back(
+    tile_ref,
+    live_ref,
+    cells_ref,
+    offsets_ref,
+    wy_high,
+    wy_low,
+    grid,
+    edge,
+    out_velocity,
+    out_affine,
+    out_offsets,
+):
     def gather(b):
-        lanes, row, cell, frac, alive = particle(b)
+        lanes, row, cell, frac, alive = particle(b, tile_ref, live_ref, cells_ref, offsets_ref)
         first = (lax.shift_right_logical(tile_ref[b], 5) & 3) * 4
         left = jnp.concatenate(
             [ref[:, pl.ds(first, 6)].reshape(144, 128) for ref in (grid, edge)], 1
@@ -472,8 +581,6 @@
         return carry
 
     lax.fori_loop(0, BLOCKS // UNROLL, gather_some, 0)
-    for send in list(edge_sends.values()) + list(class_sends.values()):
-        send.wait_send()
 
 
 def on_device(
@@ -489,43 +596,11 @@
     friction_class,
     bucket_velocity,
 ):
+    hbm = pl.BlockSpec(memory_space=pltpu.HBM)
+    vmem = pl.BlockSpec(memory_space=pltpu.VMEM)
     smem = pl.BlockSpec(memory_space=pltpu.SMEM)
-    vmem = pl.BlockSpec(memory_space=pltpu.VMEM)
     count = cells.shape[0]
-    copies = 2 * len(FACES) + len(EDGES)
-    return pl.pallas_call(
-        kernel,
-        out_shape=(
-            jax.ShapeDtypeStruct((3, count), F32),
-            jax.ShapeDtypeStruct((9, count), F32),
-            jax.ShapeDtypeStruct((3, count), F32),
-        ),
-        in_specs=[smem] * 3 + [vmem] * 8,
-        out_specs=(vmem,) * 3,
-        scratch_shapes=[
-            pltpu.VMEM((BLOCKS, 144, 256), BF16),
-            pltpu.VMEM((BLOCKS, 144, 256), BF16),
-            pltpu.VMEM((BLOCKS + 1, 3, 8, 8, 128), F32),
-            pltpu.VMEM((BLOCKS + 1, 3, 8, 8, 128), F32),
-            pltpu.VMEM((3, XP, 8, 128), F32),
-            pltpu.VMEM((3, XP, 8, 128), F32),
-            pltpu.VMEM((24, 128), F32),
-            pltpu.VMEM((2, 128, 128), F32),
-            pltpu.VMEM((2, 4, 16, 128), F32),
-            pltpu.VMEM((2, 1, 18, 8, 128), F32),
-            pltpu.VMEM((2, 3, 2, 8, 128), F32),
-            pltpu.VMEM((4, 1, 2, 8, 128), F32),
-            pltpu.VMEM((len(EDGES), 24, 128), F32),
-            pltpu.VMEM((2, 2, 1, 16, 128), F32),
-            pltpu.VMEM((2, 2, 4, 8, 128), F32),
-            pltpu.VMEM((4, 2, 1, 8, 128), F32),
-            pltpu.SemaphoreType.DMA((copies,)),
-            pltpu.SemaphoreType.DMA((copies,)),
-        ],
-        compiler_params=pltpu.CompilerParams(
-            collective_id=0, has_side_effects=True, vmem_limit_bytes=40 * 1024 * 1024
-        ),
-    )(
+    args = (
         block_tile,
         live_blocks,
         bucket_velocity,
@@ -538,6 +613,58 @@
         bucket_mask,
         friction_class,
     )
+    kept = pl.pallas_call(
+        spread,
+        out_shape=(
+            pltpu.SMEM((BLOCKS,), jnp.int32),
+            pltpu.SMEM((1,), jnp.int32),
+            pltpu.VMEM((BLOCKS, 128), jnp.int32),
+            pltpu.VMEM((3, count), F32),
+            pltpu.VMEM((BLOCKS, 144, 256), BF16),
+            pltpu.VMEM((BLOCKS, 144, 256), BF16),
+            pltpu.VMEM((3, XP, 8, 128), F32),
+            pltpu.VMEM((3, XP, 8, 128), F32),
+        ),
+        in_specs=[hbm] * len(args),
+        out_specs=(smem,) * 2 + (vmem,) * 6,
+        scratch_shapes=[pltpu.SMEM((3,), F32)]
+        + [pltpu.VMEM(arg.shape, arg.dtype) for arg in args[5:]]
+        + [
+            pltpu.VMEM((BLOCKS + 1, 3, 8, 8, 128), F32),
+            pltpu.VMEM((BLOCKS + 1, 3, 8, 8, 128), F32),
+            pltpu.VMEM((2, 8, 128), F32),
+            pltpu.VMEM((2, 8, 128), F32),
+            pltpu.VMEM((2, 128, 128), F32),
+            pltpu.VMEM((2, 4, 16, 128), F32),
+            pltpu.VMEM((2, 8, 128), F32),
+            pltpu.VMEM((8, 128), F32),
+            pltpu.VMEM((2, 18, 8, 128), F32),
+            pltpu.VMEM((2, 3, 2, 8, 128), F32),
+            pltpu.VMEM((len(FACES), 2, 8, 128), F32),
+            pltpu.VMEM((2, 8, 128), F32),
+            pltpu.VMEM((len(FACES), 2, 8, 128), F32),
+            pltpu.VMEM((2, 2, 16, 128), F32),
+            pltpu.VMEM((len(FACES), 8, 128), F32),
+            pltpu.VMEM((2, 8, 128), F32),
+            pltpu.SemaphoreType.DMA((len(args),)),
+            pltpu.SemaphoreType.DMA((SENDS,)),
+            pltpu.SemaphoreType.DMA((SENDS,)),
+        ],
+        compiler_params=pltpu.CompilerParams(
+            collective_id=0, has_side_effects=True, vmem_limit_bytes=VMEM_SPREAD
+        ),
+    )(*args)
+    return pl.pallas_call(
+        collect_back,
+        out_shape=(
+            jax.ShapeDtypeStruct((3, count), F32),
+            jax.ShapeDtypeStruct((9, count), F32),
+            jax.ShapeDtypeStruct((3, count), F32),
+        ),
+        in_specs=[smem] * 2 + [vmem] * 6,
+        out_specs=(vmem,) * 3,
+        compiler_params=pltpu.CompilerParams(vmem_limit_bytes=VMEM_COLLECT),
+    )(*kept)
 
 
 def solution(mesh):

time: 34.4 us -> 23.2 us (0.67); the launches traced: 33.9 us -> 23 us
  local copies, waits for them, and re-layouts: 8.77 us -> 0 us
  Pallas kernels: 23.8 us -> 21.8 us
    unnamed x23 -> x0, local copies, waits for them, and re-layouts: 8.77 us -> none
    pallas_call x1 -> x2, Pallas kernels: 23.8 us -> 21.8 us  [the longest x1 19.8 us: on_device(): pl.pallas_call(spread, out_shape=(pltpu.SMEM((BLOCKS,), jnp.int32), pltpu...]
where the time goes in v2:
time: 23.2 us; the launch traced here: 23 us
  Pallas kernels  21.8 us (94%)
  between operations  1.29 us (6%)
    pallas_call x1, Pallas kernels, on_device(): pl.pallas_call(spread, out_shape=(pltpu.SMEM((BLOCKS,), jnp.int32), pltpu...  19.8 us
    pallas_call x1, Pallas kernels, on_device(): pl.pallas_call(collect_back, out_shape=(jax.ShapeDtypeStruct((3, count),...  1.99 us

profile of v2, /device:TPU:1, one launch (start us, length us, event | category | flops | bytes accessed | tf_op | source)
XLA Modules:
  0.0 23.0 jit_solution(4786342260016760249)
XLA Ops:
  1.3 19.8 %shard_map.130 = (s32[16]{0:T(128)S(4)}, s32[1]{0:T(128)S(4)}, s32[16,128]{1,0:T(8,128)S(1)}, f32[3,2048]{1,0:T(4,128)S(1)}, bf16[16,144,256]{2,1,0:T(8,128)(2,1...) custom-call(s32[16]{0:T(128)} %tile_hbm.1, ...), custom_call_target="tpu_custom_call" | custom-call | tf_op jit(solution)/shard_map/pallas_call | solution.py:616
  21.0 2.0 %shard_map.131 = (f32[3,2048]{1,0:T(4,128)}, f32[9,2048]{1,0:T(8,128)}, f32[3,2048]{1,0:T(4,128)}) custom-call(s32[16]{0:T(128)S(4)} %get-tuple-element.11.tile_ref, s32[1]{0:T(128)S(4)} %get-tuple-element.12.live_ref, s32[16,128]{1,0:T(8,128)S(1)} %get-tuple-element.13.cells_ref, f32[3,2048]{1,0:T(4,128)S(1)} %get-tuple-element.14.offsets_ref, ...), custom_call_target="tpu_custom_call" | custom-call | tf_op jit(solution)/shard_map/pallas_call | solution.py:657

commit v3 on v2

v3 whole, which is shorter than its diff:
```python
import jax
import jax.numpy as jnp
from jax import lax
from jax.experimental import pallas as pl
from jax.experimental.pallas import tpu as pltpu
from jax.sharding import PartitionSpec as P

DT = 0.1
GRAVITY = -9.8
MASS_FLOOR = 0.5
SLIP_FLOOR = 0.1
FRICTION = (0.1, 0.4, 0.8, 1.2)

BLOCKS = 16
UNROLL = 8
VMEM_SPREAD = 58 * 1024 * 1024
VMEM_FINISH = 16 * 1024 * 1024
XN = 18
STEP = 20
F32 = jnp.float32
BF16 = jnp.bfloat16
MESH = pl.DeviceIdType.MESH

PLANE, LEFT, EDGE_A, FIRST, EDGE_B, RIGHT, TILES = 0, 4, 5, 7, 25, 27, 28

FACES = [(dz, dx) for dz in (-1, 0, 1) for dx in (-1, 0, 1) if (dz, dx) != (0, 0)]
NINE = [(dz, dx) for dz in (-1, 1, 0) for dx in (-1, 1, 0)]
SLOT = {side: index for index, side in enumerate(NINE)}
Z_PLANE = {-1: 0, 1: 3}
Z_PAIR = {-1: 0, 1: 2}


def spline(frac):
    weights = (
        0.5 * (1.5 - frac) * (1.5 - frac),
        0.75 - (frac - 1.0) * (frac - 1.0),
        0.5 * (frac - 0.5) * (frac - 0.5),
    )
    moments = tuple(w * (float(k) - frac) for k, w in enumerate(weights))
    return weights, moments


def pick(hits, values):
    out = jnp.where(hits[2], values[2], 0.0)
    out = jnp.where(hits[1], values[1], out)
    return jnp.where(hits[0], values[0], out)


def split(value):
    high = value.astype(BF16)
    return high, (value - high.astype(F32)).astype(BF16)


def along_z(cell, frac):
    low = lax.broadcasted_iota(jnp.int32, (8, 128), 0) & 1
    near = lax.shift_right_logical(cell, 4) - low
    weights, moments = spline(frac)
    plain, moment = [], []
    for pair in range(3):
        hits = [near == 2 * pair - k for k in range(3)]
        plain.append(pick(hits, weights))
        moment.append(pick(hits, moments))
    return plain, moment


def six(near, weights, moments):
    hits = [near == v for v in range(4)]
    plain, moment = [], []
    for i in range(6):
        outs = []
        for values in (weights, moments):
            out = jnp.zeros((8, 128), F32)
            for k in range(3):
                if 0 <= i - k < 4:
                    out = jnp.where(hits[i - k], values[k], out)
            outs.append(out)
        plain.append(outs[0])
        moment.append(outs[1])
    return plain, moment


def near_z(cell):
    return lax.shift_right_logical(cell, 4)


def near_x(cell):
    return lax.shift_right_logical(cell, 2) & 3


def along_x_rows(cell, frac):
    row = lax.broadcasted_iota(jnp.int32, (8, 128), 0)
    weights, moments = spline(frac)
    hits = [row - near_x(cell) == k for k in range(3)]
    return jnp.concatenate([pick(hits, weights), pick(hits, moments)], 1)


def along_edge(cell, frac, across):
    row = lax.broadcasted_iota(jnp.int32, (8, 128), 0)
    first = jnp.where(across == 0, 0, jnp.where(across == 31, 4, -999))
    place = (row & 1) - (cell & 3) + first
    weights, moments = spline(frac)
    hits = [place == k for k in range(3)]
    return pick(hits, weights), pick(hits, moments)


def along_y(cell, frac, first):
    row = lax.broadcasted_iota(jnp.int32, (8, 128), 0)
    diff = (cell & 3) + (first - 1) - row
    weights, moments = spline(frac)
    plain, moment = [], []
    for t in range(16):
        shifted = diff
        if t == 0:
            shifted = jnp.where(row == 0, -999, diff)
        elif t == 15:
            shifted = jnp.where(row == 7, -999, diff)
        hits = [shifted == 8 * t - k for k in range(3)]
        plain.append(pick(hits, weights))
        moment.append(pick(hits, moments))
    return jnp.concatenate([jnp.concatenate(plain, 0), jnp.concatenate(moment, 0)], 1)


def by_channel(parts):
    row = lax.broadcasted_iota(jnp.int32, (8, 128), 0)
    out = jnp.where(row < 6, parts[2], parts[3])
    out = jnp.where(row < 4, parts[1], out)
    return jnp.where(row < 2, parts[0], out)


def dot(left, right, dims):
    return lax.dot_general(left, right, (dims, ((), ())), preferred_element_type=F32)


NN = ((1,), (0,))
NT = ((1,), (1,))


def contact(mass, momentum, kind, friction, bvel):
    floor = jnp.maximum(mass, MASS_FLOOR)
    speed = [momentum[0] / floor + DT * GRAVITY, momentum[1] / floor, momentum[2] / floor]
    coeff = jnp.where(friction == 3.0, FRICTION[3], 0.0)
    for level in range(3):
        coeff = jnp.where(friction == float(level), FRICTION[level], coeff)
    rel = [speed[i] - bvel[i] for i in range(3)]
    normal = jnp.minimum(rel[0], 0.0)
    slide = jnp.sqrt(rel[1] * rel[1] + rel[2] * rel[2])
    factor = jnp.maximum(0.0, 1.0 + coeff * normal / jnp.maximum(slide, SLIP_FLOOR))
    hit = [bvel[0] + (rel[0] - normal), bvel[1] + factor * rel[1], bvel[2] + factor * rel[2]]
    return [
        jnp.where(kind == 2.0, bvel[i], jnp.where(kind == 1.0, hit[i], speed[i])) for i in range(3)
    ]


def particle(b, tile_ref, live_ref, cells_ref, offsets_ref):
    lanes = pl.ds(pl.multiple_of(b * 128, 128), 128)

    def row(ref, r):
        return jnp.broadcast_to(ref[pl.ds(r, 1), lanes], (8, 128))

    cell = jnp.broadcast_to(cells_ref[pl.ds(b, 1), :], (8, 128))
    frac = [row(offsets_ref, r) for r in range(3)]
    alive = jnp.where(b < live_ref[0], 1.0, 0.0)
    tile = tile_ref[b]
    return lanes, row, cell, frac, alive, lax.shift_right_logical(tile, 5) & 3, tile & 31


def edge_row(z):
    return 60 * (z % 2) + STEP * (z // 2)


def spread(
    tile_hbm,
    live_hbm,
    bvel_hbm,
    cells_hbm,
    offsets_hbm,
    velocity_hbm,
    affine_hbm,
    stress_hbm,
    mass_hbm,
    mask_hbm,
    friction_hbm,
    tile_ref,
    live_ref,
    cells_ref,
    offsets_ref,
    out_velocity,
    out_affine,
    out_offsets,
    edge_speed,
    bvel_ref,
    velocity_ref,
    affine_ref,
    stress_ref,
    mass_ref,
    mask_ref,
    friction_ref,
    wy,
    patch,
    grid,
    speed,
    ends,
    classes,
    planes,
    got_z,
    got_x,
    got_zx,
    got_ends,
    load_sem,
    send_sem,
    recv_sem,
):
    loads = [
        pltpu.make_async_copy(source, target, load_sem.at[index])
        for index, (source, target) in enumerate(
            (
                (cells_hbm, cells_ref),
                (offsets_hbm, offsets_ref),
                (tile_hbm, tile_ref),
                (live_hbm, live_ref),
                (mass_hbm, mass_ref),
                (velocity_hbm, velocity_ref),
                (affine_hbm, affine_ref),
                (stress_hbm, stress_ref),
                (mask_hbm, mask_ref),
                (friction_hbm, friction_ref),
                (bvel_hbm, bvel_ref),
            )
        )
    ]
    for load in loads:
        load.start()

    ix, iy, iz = lax.axis_index("gx"), lax.axis_index("gy"), lax.axis_index("gz")
    nx, ny, nz = lax.axis_size("gx"), lax.axis_size("gy"), lax.axis_size("gz")
    above, below = iz < nz - 1, iz > 0

    def device(dz, dx, dy):
        return {
            "gx": lax.rem(ix + dx + nx, nx),
            "gy": lax.rem(iy + dy + ny, ny),
            "gz": lax.rem(iz + dz + nz, nz),
        }

    def where_z(dz, action):
        if dz == 0:
            action()
        else:
            pl.when(above if dz == 1 else below)(action)

    barrier = pltpu.get_barrier_semaphore()
    for dz in (-1, 0, 1):

        def greet(dz=dz):
            for dx in (-1, 0, 1):
                for dy in (-1, 0, 1):
                    if (dz, dx, dy) != (0, 0, 0):
                        pl.semaphore_signal(
                            barrier, inc=1, device_id=device(dz, dx, dy), device_id_type=MESH
                        )

        where_z(dz, greet)

    counter = iter(range(26))

    def sender(src, dst, dz, dx, dy):
        slot = next(counter)
        return pltpu.make_async_remote_copy(
            src_ref=src,
            dst_ref=dst,
            send_sem=send_sem.at[slot],
            recv_sem=recv_sem.at[slot],
            device_id=device(dz, dx, dy),
            device_id_type=MESH,
        )

    grid_sends, end_sends = {}, {}
    for dz, dx in FACES:
        if dx == 0:
            src = grid.at[Z_PAIR[dz], pl.ds(PLANE, EDGE_B)]
            dst = got_z.at[(1 + dz) // 2]
        else:
            tiles = pl.ds(LEFT if dx == -1 else EDGE_B - 2, 5)
            if dz == 0:
                src, dst = grid.at[:, tiles], got_x.at[(1 + dx) // 2]
            else:
                src, dst = grid.at[Z_PAIR[dz], tiles], got_zx.at[1 + dz + (1 + dx) // 2]
        grid_sends[-dz, -dx] = sender(src, dst, dz, dx, 0)
    for dz, dx in NINE:
        for dy in (-1, 1):
            side = (1 + dy) // 2
            end_sends[-dz, -dx, -dy] = sender(
                ends.at[side], got_ends.at[side, SLOT[dz, dx]], dz, dx, dy
            )

    speed[...] = jnp.zeros((3, XN, 8, 128), F32)
    classes[...] = jnp.zeros((2, 128, 128), F32)
    patch[pl.ds(0, 12)] = jnp.zeros((12, 3, 8, 128), F32)

    def clear(b, carry):
        patch[pl.ds(STEP * b + 18, 14)] = jnp.zeros((14, 3, 8, 128), F32)
        return carry

    lax.fori_loop(0, BLOCKS, clear, 0)
    for load in loads[:8]:
        load.wait()

    zero = jnp.zeros((8, 128), F32)

    def scatter(b, edges):
        lanes, row, cell, frac, alive, down, across = particle(
            b, tile_ref, live_ref, cells_ref, offsets_ref
        )
        right_high, right_low = split(along_y(cell, frac[2], across * 4))
        right = jnp.concatenate([right_high, right_low], 0)
        wy[b] = right
        wz, wz_moment = along_z(cell, frac[0])
        wx, wx_moment = six(near_x(cell), *spline(frac[1]))
        mass = jnp.broadcast_to(mass_ref[pl.ds(b, 1), :], (8, 128)) * alive
        push = by_channel([mass] + [mass * row(velocity_ref, i) for i in range(3)])
        scale = 4.0 * DT * alive

        def twist(j):
            return mass * by_channel(
                [zero] + [row(affine_ref, 3 * i + j) for i in range(3)]
            ) - scale * by_channel([zero] + [row(stress_ref, 3 * i + j) for i in range(3)])

        twists = [twist(j) for j in range(3)]
        plain, moment = [], []
        for pair in range(3):
            lead = wz[pair] * push + wz_moment[pair] * twists[0]
            second = wz[pair] * twists[1]
            third = wz[pair] * twists[2]
            for i in range(6):
                plain.append(wx[i] * lead + wx_moment[i] * second)
                moment.append(wx[i] * third)
        left = jnp.concatenate([jnp.concatenate(plain, 0), jnp.concatenate(moment, 0)], 1)
        left_high, left_low = split(left)
        found = dot(left_high, right, NT)
        found = found[:, :128] + (found[:, 128:] + dot(left_low, right_high, NT))
        for pair in range(3):
            patch[pl.ds(STEP * b + 12, 6), pair] = found[48 * pair : 48 * pair + 48].reshape(
                6, 8, 128
            )

        we, we_moment = along_edge(cell, frac[2], across)
        lead = we * push + we_moment * twists[2]
        second = we * twists[0]
        third = we * twists[1]
        wz, wz_moment = six(near_z(cell), *spline(frac[0]))
        plain = [wz[z] * lead + wz_moment[z] * second for z in range(6)]
        moment = [wz[z] * third for z in range(6)]
        left = jnp.concatenate([jnp.concatenate(plain, 0), jnp.concatenate(moment, 0)], 1)
        across_x = along_x_rows(cell, frac[1])
        across_high = across_x.astype(BF16).astype(F32)
        pad = jnp.zeros((56, 256), F32)
        right = jnp.concatenate([across_high, pad, across_x - across_high, pad], 0).astype(BF16)
        found = dot(jnp.concatenate(split(left), 0), right, NT)
        found = found[:48] + found[48:]
        low = jnp.where(across == 0, 1.0, 0.0)
        high = jnp.where(across == 31, 1.0, 0.0)
        out = []
        for z in range(6):
            part = pltpu.roll(found[8 * z : 8 * z + 8], 4 * down, 1)
            out.append(edges[2 * z] + low * part)
            out.append(edges[2 * z + 1] + high * part)
        return tuple(out)

    def scatter_some(step, edges):
        for u in range(UNROLL):
            edges = scatter(step * UNROLL + u, edges)
        return edges

    edges = lax.fori_loop(0, BLOCKS // UNROLL, scatter_some, (zero,) * 12)

    lane = lax.broadcasted_iota(jnp.int32, (8, 128), 1)
    for side in range(2):
        total = zero
        for z in range(6):
            part = edges[2 * z + side]
            part = jnp.where(lane < XN, part + pltpu.roll(part, 64, 1), 0.0)
            if edge_row(z):
                part = pltpu.roll(part, edge_row(z), 1)
            total = total + part
        ends[side, 0] = total
        for pair in range(3):
            grid[pair, EDGE_A + side] = total
            grid[pair, EDGE_B + side] = total

    loads[8].wait()
    loads[9].wait()
    planes[0] = mask_ref[...].astype(F32)
    planes[1] = friction_ref[...].astype(F32)
    flat = planes.reshape(128, 128)
    for pair in range(3):
        grid[pair, LEFT] = flat[pl.ds(0, 8, stride=16), :]
        grid[pair, RIGHT] = flat[pl.ds(15, 8, stride=16), :]
    for dz in (-1, 1):
        grid[Z_PAIR[dz], pl.ds(PLANE, 4)] = planes[:, Z_PLANE[dz]].reshape(4, 8, 128)
    grid[1, pl.ds(PLANE, 4)] = jnp.zeros((4, 8, 128), F32)
    for kind in range(2):
        for z in range(4):
            classes[kind, pl.ds(edge_row(z + 1) + 1, 16), :] = planes[kind, z]
    flipped = [classes[kind].T for kind in range(2)]
    tail = jnp.zeros((6, 128), F32)
    for side, y in ((0, 0), (1, 127)):
        ends[side, 1] = jnp.concatenate([flipped[0][y : y + 1], flipped[1][y : y + 1], tail], 0)

    for pair in range(3):
        total = jnp.zeros((XN, 8, 128), F32)
        for b in range(BLOCKS):
            down = lax.shift_right_logical(tile_ref[b], 5) & 3
            total = total + patch[pl.ds(STEP * b + 12 - 4 * down, XN), pair]
        grid[pair, pl.ds(FIRST, XN)] = total

    pl.semaphore_wait(
        barrier, 26 - 9 * (1 - above.astype(jnp.int32)) - 9 * (1 - below.astype(jnp.int32))
    )
    for dz, dx in FACES:
        where_z(dz, grid_sends[-dz, -dx].start)
    for dz in (-1, 1, 0):

        def send_ends(dz=dz):
            for dx in (-1, 1, 0):
                for dy in (-1, 1):
                    end_sends[-dz, -dx, -dy].start()

        where_z(dz, send_ends)

    for pair in range(3):
        speed[pair] = grid[pair, pl.ds(FIRST, XN)]
    for dz, dx in FACES:

        def add(dz=dz, dx=dx):
            grid_sends[dz, dx].wait_recv()
            if dx == 0:
                pair = Z_PAIR[dz]
                came = got_z.at[(1 - dz) // 2]
                speed[pair] = speed[pair] + came[pl.ds(FIRST, XN)]
                z = 0 if dz == -1 else 5
                for kind in range(2):
                    classes[kind, pl.ds(edge_row(z) + 1, 16), :] = came[
                        pl.ds(PLANE + 2 * kind, 2)
                    ].reshape(16, 128)
                return
            x = 0 if dx == -1 else 17
            xs = pl.ds(8 + 8 * dx, 2)
            first, mark = (0, 4) if dx == -1 else (3, 0)
            if dz == 0:
                came = got_x.at[(1 - dx) // 2]
                speed[:, xs] = speed[:, xs] + came[:, pl.ds(first, 2)]
                tile, depths = came[0, mark], range(4)
            else:
                pair = Z_PAIR[dz]
                came = got_zx.at[1 - dz + (1 - dx) // 2]
                speed[pair, xs] = speed[pair, xs] + came[pl.ds(first, 2)]
                tile, depths = came[mark], (Z_PLANE[-dz],)
            for kind in range(2):
                for z in depths:
                    at = edge_row(z + 1 + 4 * dz) + x
                    classes[kind, pl.ds(at, 1), :] = tile[4 * kind + z : 4 * kind + z + 1]

        where_z(dz, add)

    loads[10].wait()
    bvel = [bvel_ref[i] for i in range(3)]
    rows = speed.reshape(3 * XN * 8, 128)
    for z in range(6):
        pair, low = z // 2, z % 2

        def at(c):
            return pl.ds(pair * XN * 8 + 2 * c + low, XN, stride=8)

        load = [rows[at(c), :] for c in range(4)]
        kinds = [classes[kind, pl.ds(edge_row(z), XN), :] for kind in range(2)]
        new = contact(load[0], load[1:], kinds[0], kinds[1], bvel)
        for i in range(3):
            value = new[i]
            if z == 0:
                value = jnp.where(below, value, 0.0)
            elif z == 5:
                value = jnp.where(above, value, 0.0)
            rows[at(i + 1), :] = value

    def gather(b):
        lanes, row, cell, frac, alive, down, across = particle(
            b, tile_ref, live_ref, cells_ref, offsets_ref
        )
        left_high, left_low = split(speed[:, pl.ds(4 * down, 6)].reshape(144, 128))
        right_high, right_low = wy[b, pl.ds(0, 128)], wy[b, pl.ds(128, 128)]
        found = dot(
            jnp.concatenate([left_high, left_low], 1),
            jnp.concatenate([right_high, right_high], 0),
            NN,
        ) + dot(left_high, right_low, NN)
        plain = found[:, :128].reshape(3, 6, 8, 128)
        moment = found[:, 128:].reshape(3, 6, 8, 128)
        wz, wz_moment = along_z(cell, frac[0])
        wx, wx_moment = six(near_x(cell), *spline(frac[1]))
        totals = [zero] * 4
        for pair in range(3):
            sum_w = sum(wx[i] * plain[pair, i] for i in range(6))
            sum_x = sum(wx_moment[i] * plain[pair, i] for i in range(6))
            sum_y = sum(wx[i] * moment[pair, i] for i in range(6))
            totals[0] = totals[0] + wz[pair] * sum_w
            totals[1] = totals[1] + wz_moment[pair] * sum_w
            totals[2] = totals[2] + wz[pair] * sum_x
            totals[3] = totals[3] + wz[pair] * sum_y
        totals = [(t + pltpu.roll(t, 7, 0)) * alive for t in totals]
        for i in range(3):
            here = 2 * i + 2
            moved = totals[0][here : here + 1]
            out_velocity[pl.ds(i, 1), lanes] = moved
            out_offsets[pl.ds(i, 1), lanes] = frac[i][:1] * alive + DT * moved
            for j in range(3):
                out_affine[pl.ds(3 * i + j, 1), lanes] = 4.0 * totals[j + 1][here : here + 1]

    def gather_some(step, carry):
        for u in range(UNROLL):
            gather(step * UNROLL + u)
        return carry

    lax.fori_loop(0, BLOCKS // UNROLL, gather_some, 0)

    flipped = [classes[kind].T for kind in range(2)]
    half = jnp.where(lane >= 60, lane - 60, lane)
    pair = jnp.where(half >= 2 * STEP, 2, jnp.where(half >= STEP, 1, 0))
    place = half - STEP * pair
    inner = lane < 120
    totals = [ends[0, 0], ends[1, 0]]
    marks = [zero, zero]
    for dz, dx in NINE:
        keep = inner
        if dx == -1:
            keep = keep & (place < 2)
        elif dx == 1:
            keep = keep & (place >= 16) & (place < 18)
        if dz == -1:
            keep = keep & (pair == 0) & below
        elif dz == 1:
            keep = keep & (pair == 2) & above
        shift = (16 * dx + 2 * STEP * dz) % 128

        def moved(value):
            return jnp.where(keep, pltpu.roll(value, shift, 1) if shift else value, 0.0)

        if (dz, dx) != (0, 0):
            for side in range(2):
                if dx == 0:
                    came = got_z[(1 - dz) // 2, EDGE_A + side]
                else:
                    tile = (2 if dx == -1 else 1) + side
                    if dz == 0:
                        came = got_x[(1 - dx) // 2, 0, tile]
                    else:
                        came = got_zx[1 - dz + (1 - dx) // 2, tile]
                totals[side] = totals[side] + moved(came)
        for dy in (-1, 1):
            where_z(dz, end_sends[dz, dx, dy].wait_recv)
            side = (1 + dy) // 2
            came = got_ends.at[1 - side, SLOT[-dz, -dx]]
            totals[side] = totals[side] + moved(came[0])
            marks[side] = marks[side] + moved(came[1])
    kinds = [
        jnp.concatenate(
            [
                marks[0][kind : kind + 1],
                flipped[kind][0:1],
                flipped[kind][127:128],
                marks[1][kind : kind + 1],
            ],
            0,
        )
        for kind in range(2)
    ]
    parts = [
        jnp.concatenate([totals[0][2 * c : 2 * c + 2], totals[1][2 * c : 2 * c + 2]], 0)
        for c in range(4)
    ]
    new = contact(parts[0], parts[1:], kinds[0], kinds[1], bvel)
    first_row, last_row = edge_row(0), edge_row(5)
    here = lane[:4]
    outside = ((here < first_row + STEP) & (iz == 0)) | ((here >= last_row) & (iz == nz - 1))
    new = [jnp.where(outside, 0.0, value) for value in new]
    for side in range(2):
        edge_speed[side] = jnp.concatenate(
            [jnp.zeros((2, 128), F32)] + [value[2 * side : 2 * side + 2] for value in new], 0
        )

    for dz in (-1, 0, 1):

        def finish(dz=dz):
            for dx in (-1, 0, 1):
                if (dz, dx) != (0, 0):
                    grid_sends[-dz, -dx].wait_send()
                for dy in (-1, 1):
                    end_sends[-dz, -dx, -dy].wait_send()

        where_z(dz, finish)


def finish(
    tile_ref,
    live_ref,
    cells_ref,
    offsets_ref,
    velocity_ref,
    affine_ref,
    moved_ref,
    edge_speed,
    out_velocity,
    out_affine,
    out_offsets,
):
    out_velocity[...] = velocity_ref[...]
    out_affine[...] = affine_ref[...]
    out_offsets[...] = moved_ref[...]

    def one(b, carry):
        across = tile_ref[b] & 31

        @pl.when((across == 0) | (across == 31))
        def _():
            lanes, row, cell, frac, alive, down, across = particle(
                b, tile_ref, live_ref, cells_ref, offsets_ref
            )
            side = jnp.where(across == 0, 0, 1)
            value = edge_speed[side]
            left = jnp.concatenate(
                [pltpu.roll(value, (128 - edge_row(z) - 4 * down) & 127, 1) for z in range(6)], 0
            )
            left_high, left_low = split(left)
            right = jnp.concatenate(
                [along_x_rows(cell, frac[1]), jnp.zeros((120, 256), F32)], 0
            )
            right_high, right_low = split(right)
            found = dot(left_high, right_high, NN) + (
                dot(left_low, right_high, NN) + dot(left_high, right_low, NN)
            )
            we, we_moment = along_edge(cell, frac[2], across)
            wz, wz_moment = six(near_z(cell), *spline(frac[0]))
            sum_w = sum(wz[z] * found[8 * z : 8 * z + 8, :128] for z in range(6))
            sum_z = sum(wz_moment[z] * found[8 * z : 8 * z + 8, :128] for z in range(6))
            sum_x = sum(wz[z] * found[8 * z : 8 * z + 8, 128:] for z in range(6))
            totals = [we * sum_w, we * sum_z, we * sum_x, we_moment * sum_w]
            totals = [(t + pltpu.roll(t, 7, 0)) * alive for t in totals]
            for i in range(3):
                here = 2 * i + 2
                moved = totals[0][here : here + 1]
                out_velocity[pl.ds(i, 1), lanes] += moved
                out_offsets[pl.ds(i, 1), lanes] += DT * moved
                for j in range(3):
                    out_affine[pl.ds(3 * i + j, 1), lanes] += (
                        4.0 * totals[j + 1][here : here + 1]
                    )

        return carry

    lax.fori_loop(0, BLOCKS, one, 0)


def on_device(
    cells,
    offsets,
    velocity,
    affine,
    stress,
    mass,
    block_tile,
    live_blocks,
    bucket_mask,
    friction_class,
    bucket_velocity,
):
    hbm = pl.BlockSpec(memory_space=pltpu.HBM)
    vmem = pl.BlockSpec(memory_space=pltpu.VMEM)
    smem = pl.BlockSpec(memory_space=pltpu.SMEM)
    count = cells.shape[0]
    args = (
        block_tile,
        live_blocks,
        bucket_velocity,
        cells.reshape(BLOCKS, 128),
        offsets,
        velocity,
        affine,
        stress,
        mass.reshape(BLOCKS, 128),
        bucket_mask,
        friction_class,
    )
    kept = pl.pallas_call(
        spread,
        out_shape=(
            pltpu.SMEM((BLOCKS,), jnp.int32),
            pltpu.SMEM((1,), jnp.int32),
            pltpu.VMEM((BLOCKS, 128), jnp.int32),
            pltpu.VMEM((3, count), F32),
            pltpu.VMEM((3, count), F32),
            pltpu.VMEM((9, count), F32),
            pltpu.VMEM((3, count), F32),
            pltpu.VMEM((2, 8, 128), F32),
        ),
        in_specs=[hbm] * len(args),
        out_specs=(smem,) * 2 + (vmem,) * 6,
        scratch_shapes=[pltpu.SMEM((3,), F32)]
        + [pltpu.VMEM(arg.shape, arg.dtype) for arg in args[5:]]
        + [
            pltpu.VMEM((BLOCKS, 256, 256), BF16),
            pltpu.VMEM((STEP * BLOCKS + 12, 3, 8, 128), F32),
            pltpu.VMEM((3, TILES, 8, 128), F32),
            pltpu.VMEM((3, XN, 8, 128), F32),
            pltpu.VMEM((2, 2, 8, 128), F32),
            pltpu.VMEM((2, 128, 128), F32),
            pltpu.VMEM((2, 4, 16, 128), F32),
            pltpu.VMEM((2, EDGE_B, 8, 128), F32),
            pltpu.VMEM((2, 3, 5, 8, 128), F32),
            pltpu.VMEM((4, 5, 8, 128), F32),
            pltpu.VMEM((2, len(NINE), 2, 8, 128), F32),
            pltpu.SemaphoreType.DMA((len(args),)),
            pltpu.SemaphoreType.DMA((26,)),
            pltpu.SemaphoreType.DMA((26,)),
        ],
        compiler_params=pltpu.CompilerParams(
            collective_id=0, has_side_effects=True, vmem_limit_bytes=VMEM_SPREAD
        ),
    )(*args)
    return pl.pallas_call(
        finish,
        out_shape=(
            jax.ShapeDtypeStruct((3, count), F32),
            jax.ShapeDtypeStruct((9, count), F32),
            jax.ShapeDtypeStruct((3, count), F32),
        ),
        in_specs=[smem] * 2 + [vmem] * 6,
        out_specs=(vmem,) * 3,
        compiler_params=pltpu.CompilerParams(vmem_limit_bytes=VMEM_FINISH),
    )(*kept)


def solution(mesh):
    along = ("gx", "gy", "gz")
    return jax.shard_map(
        on_device,
        mesh=mesh,
        in_specs=(
            P(along),
            P(None, along),
            P(None, along),
            P(None, along),
            P(None, along),
            P(along),
            P(along),
            P(along),
            P("gz", "gx", "gy"),
            P("gz", "gx", "gy"),
            P(),
        ),
        out_specs=(P(None, along), P(None, along), P(None, along)),
        check_vma=False,
    )
```

time: 23.2 us -> 23.4 us (level)
    pallas_call x1, Pallas kernels: 19.8 us -> 20.5 us  [on_device(): pl.pallas_call(spread, out_shape=(pltpu.SMEM((BLOCKS,), jnp.int32), pltpu...]
    pallas_call x1, Pallas kernels: 1.99 us -> 1.39 us  [on_device(): pl.pallas_call(finish, out_shape=(jax.ShapeDtypeStruct((3, count), F32),...]
where the time goes in v3:
time: 23.4 us; the launch traced here: 23.2 us
  Pallas kernels  21.9 us (94%)
  between operations  1.29 us (6%)
    pallas_call x1, Pallas kernels, on_device(): pl.pallas_call(spread, out_shape=(pltpu.SMEM((BLOCKS,), jnp.int32), pltpu...  20.5 us
    pallas_call x1, Pallas kernels, on_device(): pl.pallas_call(finish, out_shape=(jax.ShapeDtypeStruct((3, count), F32),...  1.39 us

profile of v3, /device:TPU:1, one launch (start us, length us, event | category | flops | bytes accessed | tf_op | source)
XLA Modules:
  0.0 23.2 jit_solution(17814196945562723264)
XLA Ops:
  1.3 20.5 %shard_map.130 = (s32[16]{0:T(128)S(4)}, s32[1]{0:T(128)S(4)}, s32[16,128]{1,0:T(8,128)S(1)}, f32[3,2048]{1,0:T(4,128)S(1)}, f32[3,2048]{1,0:T(4,128)S(1)}, /*in...) custom-call(s32[16]{0:T(128)} %tile_hbm.1, s32[1]{0:T(128)S(6)} %copy.14.live_hbm, f32[3]{0:T(128)} %bvel_hbm.1, ...), custom_call_target="tpu_custom_call" | custom-call | tf_op jit(solution)/shard_map/pallas_call | solution.py:692
  21.8 1.4 %shard_map.131 = (f32[3,2048]{1,0:T(4,128)}, f32[9,2048]{1,0:T(8,128)}, f32[3,2048]{1,0:T(4,128)}) custom-call(s32[16]{0:T(128)S(4)} %get-tuple-element.11.tile_ref, s32[1]{0:T(128)S(4)} %get-tuple-element.12.live_ref, s32[16,128]{1,0:T(8,128)S(1)} %get-tuple-element.13.cells_ref, f32[3,2048]{1,0:T(4,128)S(1)} %get-tuple-element.14.offsets_ref, ...), custom_call_target="tpu_custom_call" | custom-call | tf_op jit(solution)/shard_map/pallas_call | solution.py:728

commit v4 on v3

--- a/solution.py
+++ b/solution.py
@@ -21,7 +21,7 @@
 BF16 = jnp.bfloat16
 MESH = pl.DeviceIdType.MESH
 
-PLANE, LEFT, EDGE_A, FIRST, EDGE_B, RIGHT, TILES = 0, 4, 5, 7, 25, 27, 28
+PLANE, LEFT, EDGE_A, FIRST, EDGE_B, RIGHT, TILES = 0, 4, 5, 6, 24, 25, 26
 
 FACES = [(dz, dx) for dz in (-1, 0, 1) for dx in (-1, 0, 1) if (dz, dx) != (0, 0)]
 NINE = [(dz, dx) for dz in (-1, 1, 0) for dx in (-1, 1, 0)]
@@ -198,8 +198,10 @@
     wy,
     patch,
     grid,
+    across_x,
     speed,
     ends,
+    ends_z,
     classes,
     planes,
     got_z,
@@ -228,9 +230,6 @@
             )
         )
     ]
-    for load in loads:
-        load.start()
-
     ix, iy, iz = lax.axis_index("gx"), lax.axis_index("gy"), lax.axis_index("gz")
     nx, ny, nz = lax.axis_size("gx"), lax.axis_size("gy"), lax.axis_size("gz")
     above, below = iz < nz - 1, iz > 0
@@ -249,17 +248,21 @@
             pl.when(above if dz == 1 else below)(action)
 
     barrier = pltpu.get_barrier_semaphore()
-    for dz in (-1, 0, 1):
-
-        def greet(dz=dz):
-            for dx in (-1, 0, 1):
-                for dy in (-1, 0, 1):
-                    if (dz, dx, dy) != (0, 0, 0):
-                        pl.semaphore_signal(
-                            barrier, inc=1, device_id=device(dz, dx, dy), device_id_type=MESH
-                        )
-
-        where_z(dz, greet)
+
+    def greet(dz, dys):
+        for dy in dys:
+            for dx in (-1, 1, 0):
+                if (dz, dx, dy) != (0, 0, 0):
+                    pl.semaphore_signal(
+                        barrier, inc=1, device_id=device(dz, dx, dy), device_id_type=MESH
+                    )
+
+    for dz in (1, 0, -1):
+        where_z(dz, lambda dz=dz: greet(dz, (1,)))
+    for load in loads:
+        load.start()
+    for dz in (1, 0, -1):
+        where_z(dz, lambda dz=dz: greet(dz, (-1, 0)))
 
     counter = iter(range(26))
 
@@ -276,22 +279,25 @@
 
     grid_sends, end_sends = {}, {}
     for dz, dx in FACES:
-        if dx == 0:
+        if dz == 0:
+            side = (1 + dx) // 2
+            src, dst = across_x.at[side], got_x.at[side]
+        elif dx == 0:
             src = grid.at[Z_PAIR[dz], pl.ds(PLANE, EDGE_B)]
             dst = got_z.at[(1 + dz) // 2]
         else:
-            tiles = pl.ds(LEFT if dx == -1 else EDGE_B - 2, 5)
-            if dz == 0:
-                src, dst = grid.at[:, tiles], got_x.at[(1 + dx) // 2]
-            else:
-                src, dst = grid.at[Z_PAIR[dz], tiles], got_zx.at[1 + dz + (1 + dx) // 2]
+            src = grid.at[Z_PAIR[dz], pl.ds(LEFT if dx == -1 else EDGE_B - 2, 4)]
+            dst = got_zx.at[1 + dz + (1 + dx) // 2]
         grid_sends[-dz, -dx] = sender(src, dst, dz, dx, 0)
     for dz, dx in NINE:
         for dy in (-1, 1):
             side = (1 + dy) // 2
-            end_sends[-dz, -dx, -dy] = sender(
-                ends.at[side], got_ends.at[side, SLOT[dz, dx]], dz, dx, dy
-            )
+            if dz == 0:
+                src, dst = ends.at[side], got_ends.at[side, SLOT[dz, dx]]
+            else:
+                src = ends_z.at[(1 + dz) // 2, side]
+                dst = got_ends.at[side, SLOT[dz, dx], 0]
+            end_sends[-dz, -dx, -dy] = sender(src, dst, dz, dx, dy)
 
     speed[...] = jnp.zeros((3, XN, 8, 128), F32)
     classes[...] = jnp.zeros((2, 128, 128), F32)
@@ -374,6 +380,10 @@
     edges = lax.fori_loop(0, BLOCKS // UNROLL, scatter_some, (zero,) * 12)
 
     lane = lax.broadcasted_iota(jnp.int32, (8, 128), 1)
+    half = jnp.where(lane >= 60, lane - 60, lane)
+    pair_of = jnp.where(half >= 2 * STEP, 2, jnp.where(half >= STEP, 1, 0))
+    place = half - STEP * pair_of
+
     for side in range(2):
         total = zero
         for z in range(6):
@@ -383,21 +393,13 @@
                 part = pltpu.roll(part, edge_row(z), 1)
             total = total + part
         ends[side, 0] = total
-        for pair in range(3):
-            grid[pair, EDGE_A + side] = total
-            grid[pair, EDGE_B + side] = total
 
     loads[8].wait()
     loads[9].wait()
     planes[0] = mask_ref[...].astype(F32)
     planes[1] = friction_ref[...].astype(F32)
     flat = planes.reshape(128, 128)
-    for pair in range(3):
-        grid[pair, LEFT] = flat[pl.ds(0, 8, stride=16), :]
-        grid[pair, RIGHT] = flat[pl.ds(15, 8, stride=16), :]
-    for dz in (-1, 1):
-        grid[Z_PAIR[dz], pl.ds(PLANE, 4)] = planes[:, Z_PLANE[dz]].reshape(4, 8, 128)
-    grid[1, pl.ds(PLANE, 4)] = jnp.zeros((4, 8, 128), F32)
+    sides = [flat[pl.ds(0, 8, stride=16), :], flat[pl.ds(15, 8, stride=16), :]]
     for kind in range(2):
         for z in range(4):
             classes[kind, pl.ds(edge_row(z + 1) + 1, 16), :] = planes[kind, z]
@@ -406,29 +408,56 @@
     for side, y in ((0, 0), (1, 127)):
         ends[side, 1] = jnp.concatenate([flipped[0][y : y + 1], flipped[1][y : y + 1], tail], 0)
 
+    for dz in (-1, 1):
+        pair = Z_PAIR[dz]
+        grid[pair, pl.ds(PLANE, 4)] = planes[:, Z_PLANE[dz]].reshape(4, 8, 128)
+        grid[pair, LEFT] = sides[0]
+        grid[pair, RIGHT] = sides[1]
+        here = pair_of == pair
+        shift = (-STEP * dz) % 128
+
+        def beside(first, second):
+            moved = pltpu.roll(jnp.where(here, second, 0.0), shift, 1)
+            return jnp.where(here, first, 0.0) + moved
+
+        both = beside(ends[0, 0], ends[1, 0])
+        grid[pair, EDGE_A] = both
+        grid[pair, EDGE_B] = both
+        for side in range(2):
+            ends_z[(1 + dz) // 2, side] = beside(ends[side, 0], ends[side, 1])
+    for side in range(2):
+        across_x[side, 6] = ends[0, 0]
+        across_x[side, 7] = ends[1, 0]
+        across_x[side, 8] = sides[side]
+
     for pair in range(3):
         total = jnp.zeros((XN, 8, 128), F32)
         for b in range(BLOCKS):
             down = lax.shift_right_logical(tile_ref[b], 5) & 3
             total = total + patch[pl.ds(STEP * b + 12 - 4 * down, XN), pair]
         grid[pair, pl.ds(FIRST, XN)] = total
+        speed[pair] = total
+        across_x[0, pl.ds(2 * pair, 2)] = total[:2]
+        across_x[1, pl.ds(2 * pair, 2)] = total[16:]
 
     pl.semaphore_wait(
         barrier, 26 - 9 * (1 - above.astype(jnp.int32)) - 9 * (1 - below.astype(jnp.int32))
     )
+    def send_ends(dy):
+        for dz in (1, -1, 0):
+
+            def start(dz=dz):
+                for dx in (1, -1, 0):
+                    end_sends[-dz, -dx, -dy].start()
+
+            where_z(dz, start)
+
+    pl.when(iy == ny - 1)(lambda: send_ends(1))
     for dz, dx in FACES:
         where_z(dz, grid_sends[-dz, -dx].start)
-    for dz in (-1, 1, 0):
-
-        def send_ends(dz=dz):
-            for dx in (-1, 1, 0):
-                for dy in (-1, 1):
-                    end_sends[-dz, -dx, -dy].start()
-
-        where_z(dz, send_ends)
-
-    for pair in range(3):
-        speed[pair] = grid[pair, pl.ds(FIRST, XN)]
+    pl.when(iy != ny - 1)(lambda: send_ends(1))
+    send_ends(-1)
+
     for dz, dx in FACES:
 
         def add(dz=dz, dx=dx):
@@ -445,11 +474,11 @@
                 return
             x = 0 if dx == -1 else 17
             xs = pl.ds(8 + 8 * dx, 2)
-            first, mark = (0, 4) if dx == -1 else (3, 0)
+            first, mark = (0, 3) if dx == -1 else (2, 0)
             if dz == 0:
                 came = got_x.at[(1 - dx) // 2]
-                speed[:, xs] = speed[:, xs] + came[:, pl.ds(first, 2)]
-                tile, depths = came[0, mark], range(4)
+                speed[:, xs] = speed[:, xs] + came[pl.ds(0, 6)].reshape(3, 2, 8, 128)
+                tile, depths = came[8], range(4)
             else:
                 pair = Z_PAIR[dz]
                 came = got_zx.at[1 - dz + (1 - dx) // 2]
@@ -523,9 +552,6 @@
     lax.fori_loop(0, BLOCKS // UNROLL, gather_some, 0)
 
     flipped = [classes[kind].T for kind in range(2)]
-    half = jnp.where(lane >= 60, lane - 60, lane)
-    pair = jnp.where(half >= 2 * STEP, 2, jnp.where(half >= STEP, 1, 0))
-    place = half - STEP * pair
     inner = lane < 120
     totals = [ends[0, 0], ends[1, 0]]
     marks = [zero, zero]
@@ -536,31 +562,31 @@
         elif dx == 1:
             keep = keep & (place >= 16) & (place < 18)
         if dz == -1:
-            keep = keep & (pair == 0) & below
+            keep = keep & (pair_of == 0) & below
         elif dz == 1:
-            keep = keep & (pair == 2) & above
-        shift = (16 * dx + 2 * STEP * dz) % 128
-
-        def moved(value):
-            return jnp.where(keep, pltpu.roll(value, shift, 1) if shift else value, 0.0)
-
-        if (dz, dx) != (0, 0):
+            keep = keep & (pair_of == 2) & above
+        shift = 16 * dx + 2 * STEP * dz
+
+        def moved(value, second=False):
+            shift_by = (shift - STEP * dz if second else shift) % 128
+            return jnp.where(keep, pltpu.roll(value, shift_by, 1) if shift_by else value, 0.0)
+
+        if dz:
+            if dx == 0:
+                came = got_z[(1 - dz) // 2, EDGE_A]
+            else:
+                came = got_zx[1 - dz + (1 - dx) // 2, 2 if dx == -1 else 1]
+            totals[0] = totals[0] + moved(came)
+            totals[1] = totals[1] + moved(came, True)
+        elif dx:
             for side in range(2):
-                if dx == 0:
-                    came = got_z[(1 - dz) // 2, EDGE_A + side]
-                else:
-                    tile = (2 if dx == -1 else 1) + side
-                    if dz == 0:
-                        came = got_x[(1 - dx) // 2, 0, tile]
-                    else:
-                        came = got_zx[1 - dz + (1 - dx) // 2, tile]
-                totals[side] = totals[side] + moved(came)
+                totals[side] = totals[side] + moved(got_x[(1 - dx) // 2, 6 + side])
         for dy in (-1, 1):
             where_z(dz, end_sends[dz, dx, dy].wait_recv)
             side = (1 + dy) // 2
             came = got_ends.at[1 - side, SLOT[-dz, -dx]]
             totals[side] = totals[side] + moved(came[0])
-            marks[side] = marks[side] + moved(came[1])
+            marks[side] = marks[side] + (moved(came[0], True) if dz else moved(came[1]))
     kinds = [
         jnp.concatenate(
             [
@@ -709,13 +735,15 @@
             pltpu.VMEM((BLOCKS, 256, 256), BF16),
             pltpu.VMEM((STEP * BLOCKS + 12, 3, 8, 128), F32),
             pltpu.VMEM((3, TILES, 8, 128), F32),
+            pltpu.VMEM((2, 9, 8, 128), F32),
             pltpu.VMEM((3, XN, 8, 128), F32),
+            pltpu.VMEM((2, 2, 8, 128), F32),
             pltpu.VMEM((2, 2, 8, 128), F32),
             pltpu.VMEM((2, 128, 128), F32),
             pltpu.VMEM((2, 4, 16, 128), F32),
             pltpu.VMEM((2, EDGE_B, 8, 128), F32),
-            pltpu.VMEM((2, 3, 5, 8, 128), F32),
-            pltpu.VMEM((4, 5, 8, 128), F32),
+            pltpu.VMEM((2, 9, 8, 128), F32),
+            pltpu.VMEM((4, 4, 8, 128), F32),
             pltpu.VMEM((2, len(NINE), 2, 8, 128), F32),
             pltpu.SemaphoreType.DMA((len(args),)),
             pltpu.SemaphoreType.DMA((26,)),

time: 23.4 us -> 22.1 us (0.944)
  Pallas kernels: 21.9 us -> 20.7 us
    pallas_call x1, Pallas kernels: 20.5 us -> 19.5 us  [on_device(): pl.pallas_call(spread, out_shape=(pltpu.SMEM((BLOCKS,), jnp.int32), pltpu...]
where the time goes in v4:
time: 22.1 us; the launch traced here: 22 us
  Pallas kernels  20.7 us (94%)
  between operations  1.29 us (6%)
    pallas_call x1, Pallas kernels, on_device(): pl.pallas_call(spread, out_shape=(pltpu.SMEM((BLOCKS,), jnp.int32), pltpu...  19.5 us
    pallas_call x1, Pallas kernels, on_device(): pl.pallas_call(finish, out_shape=(jax.ShapeDtypeStruct((3, count), F32),...  1.16 us

profile of v4, /device:TPU:1, one launch (start us, length us, event | category | flops | bytes accessed | tf_op | source)
XLA Modules:
  0.0 22.0 jit_solution(15038087115396438568)
XLA Ops:
  1.3 19.5 %shard_map.130 = (s32[16]{0:T(128)S(4)}, s32[1]{0:T(128)S(4)}, s32[16,128]{1,0:T(8,128)S(1)}, f32[3,2048]{1,0:T(4,128)S(1)}, f32[3,2048]{1,0:T(4,128)S(1)}, /*in...) custom-call(s32[16]{0:T(128)} %tile_hbm.1, s32[1]{0:T(128)S(6)} %copy.14.live_hbm, f32[3]{0:T(128)} %bvel_hbm.1, ...), custom_call_target="tpu_custom_call" | custom-call | tf_op jit(solution)/shard_map/pallas_call | solution.py:718
  20.8 1.2 %shard_map.131 = (f32[3,2048]{1,0:T(4,128)}, f32[9,2048]{1,0:T(8,128)}, f32[3,2048]{1,0:T(4,128)}) custom-call(s32[16]{0:T(128)S(4)} %get-tuple-element.11.tile_ref, s32[1]{0:T(128)S(4)} %get-tuple-element.12.live_ref, s32[16,128]{1,0:T(8,128)S(1)} %get-tuple-element.13.cells_ref, f32[3,2048]{1,0:T(4,128)S(1)} %get-tuple-element.14.offsets_ref, ...), custom_call_target="tpu_custom_call" | custom-call | tf_op jit(solution)/shard_map/pallas_call | solution.py:756

commit v5 on v4

--- a/solution.py
+++ b/solution.py
@@ -12,7 +12,7 @@
 FRICTION = (0.1, 0.4, 0.8, 1.2)
 
 BLOCKS = 16
-UNROLL = 8
+UNROLL = 16
 VMEM_SPREAD = 58 * 1024 * 1024
 VMEM_FINISH = 16 * 1024 * 1024
 XN = 18
@@ -103,21 +103,14 @@
     return pick(hits, weights), pick(hits, moments)
 
 
-def along_y(cell, frac, first):
+def along_y(cell, frac, across):
     row = lax.broadcasted_iota(jnp.int32, (8, 128), 0)
-    diff = (cell & 3) + (first - 1) - row
+    first = jnp.where(across == 0, 2, 0)
+    last = jnp.where(across == 31, 4, 6)
+    place = jnp.where((row >= first) & (row < last), row - (cell & 3), -9)
     weights, moments = spline(frac)
-    plain, moment = [], []
-    for t in range(16):
-        shifted = diff
-        if t == 0:
-            shifted = jnp.where(row == 0, -999, diff)
-        elif t == 15:
-            shifted = jnp.where(row == 7, -999, diff)
-        hits = [shifted == 8 * t - k for k in range(3)]
-        plain.append(pick(hits, weights))
-        moment.append(pick(hits, moments))
-    return jnp.concatenate([jnp.concatenate(plain, 0), jnp.concatenate(moment, 0)], 1)
+    hits = [place == k for k in range(3)]
+    return pick(hits, weights), pick(hits, moments)
 
 
 def by_channel(parts):
@@ -162,6 +155,27 @@
     alive = jnp.where(b < live_ref[0], 1.0, 0.0)
     tile = tile_ref[b]
     return lanes, row, cell, frac, alive, lax.shift_right_logical(tile, 5) & 3, tile & 31
+
+
+def place_of(down, across):
+    return (32 * down + 4 * across + 127) & 127
+
+
+def weights_xy(cell, frac, across):
+    weights, moments = spline(frac[1])
+    wx, wx_moment = six(near_x(cell), weights, moments)
+    wy, wy_moment = along_y(cell, frac[2], across)
+    value = jnp.concatenate(
+        [
+            jnp.concatenate([wx[i] * wy for i in range(6)], 0),
+            jnp.concatenate([wx_moment[i] * wy for i in range(6)], 0),
+            jnp.concatenate([wx[i] * wy_moment for i in range(6)], 0),
+        ],
+        1,
+    )
+    high, low = split(value)
+    pad = jnp.zeros((16, 384), BF16)
+    return jnp.concatenate([high, pad, low, pad], 0)
 
 
 def edge_row(z):
@@ -188,6 +202,7 @@
     out_affine,
     out_offsets,
     edge_speed,
+    listed,
     bvel_ref,
     velocity_ref,
     affine_ref,
@@ -195,7 +210,7 @@
     mass_ref,
     mask_ref,
     friction_ref,
-    wy,
+    weights,
     patch,
     grid,
     across_x,
@@ -312,16 +327,15 @@
         load.wait()
 
     zero = jnp.zeros((8, 128), F32)
+    lane = lax.broadcasted_iota(jnp.int32, (8, 128), 1)
 
     def scatter(b, edges):
         lanes, row, cell, frac, alive, down, across = particle(
             b, tile_ref, live_ref, cells_ref, offsets_ref
         )
-        right_high, right_low = split(along_y(cell, frac[2], across * 4))
-        right = jnp.concatenate([right_high, right_low], 0)
-        wy[b] = right
+        right = weights_xy(cell, frac, across)
+        weights[b] = right
         wz, wz_moment = along_z(cell, frac[0])
-        wx, wx_moment = six(near_x(cell), *spline(frac[1]))
         mass = jnp.broadcast_to(mass_ref[pl.ds(b, 1), :], (8, 128)) * alive
         push = by_channel([mass] + [mass * row(velocity_ref, i) for i in range(3)])
         scale = 4.0 * DT * alive
@@ -332,22 +346,24 @@
             ) - scale * by_channel([zero] + [row(stress_ref, 3 * i + j) for i in range(3)])
 
         twists = [twist(j) for j in range(3)]
-        plain, moment = [], []
+        left = jnp.concatenate(
+            [
+                jnp.concatenate([wz[p] * push + wz_moment[p] * twists[0] for p in range(3)], 0),
+                jnp.concatenate([wz[p] * twists[1] for p in range(3)], 0),
+                jnp.concatenate([wz[p] * twists[2] for p in range(3)], 0),
+            ],
+            1,
+        )
+        found = dot(jnp.concatenate(split(left), 0), right, NT)
+        found = found[:24] + found[24:]
+        start = place_of(down, across)
+        group = lax.shift_right_logical((lane - start) & 127, 3)
         for pair in range(3):
-            lead = wz[pair] * push + wz_moment[pair] * twists[0]
-            second = wz[pair] * twists[1]
-            third = wz[pair] * twists[2]
+            part = found[8 * pair : 8 * pair + 8]
+            part = jnp.where(lane < 48, part + pltpu.roll(part, 64, 1), 0.0)
+            part = pltpu.roll(part, start, 1)
             for i in range(6):
-                plain.append(wx[i] * lead + wx_moment[i] * second)
-                moment.append(wx[i] * third)
-        left = jnp.concatenate([jnp.concatenate(plain, 0), jnp.concatenate(moment, 0)], 1)
-        left_high, left_low = split(left)
-        found = dot(left_high, right, NT)
-        found = found[:, :128] + (found[:, 128:] + dot(left_low, right_high, NT))
-        for pair in range(3):
-            patch[pl.ds(STEP * b + 12, 6), pair] = found[48 * pair : 48 * pair + 48].reshape(
-                6, 8, 128
-            )
+                patch[STEP * b + 12 + i, pair] = jnp.where(group == i, part, 0.0)
 
         we, we_moment = along_edge(cell, frac[2], across)
         lead = we * push + we_moment * twists[2]
@@ -379,7 +395,6 @@
 
     edges = lax.fori_loop(0, BLOCKS // UNROLL, scatter_some, (zero,) * 12)
 
-    lane = lax.broadcasted_iota(jnp.int32, (8, 128), 1)
     half = jnp.where(lane >= 60, lane - 60, lane)
     pair_of = jnp.where(half >= 2 * STEP, 2, jnp.where(half >= STEP, 1, 0))
     place = half - STEP * pair_of
@@ -396,17 +411,36 @@
 
     loads[8].wait()
     loads[9].wait()
-    planes[0] = mask_ref[...].astype(F32)
-    planes[1] = friction_ref[...].astype(F32)
+    flipped = []
+    for kind, source in enumerate((mask_ref, friction_ref)):
+        for z in range(4):
+            value = source[z].astype(F32)
+            classes[kind, pl.ds(edge_row(z + 1) + 1, 16), :] = value
+            planes[kind, z] = pltpu.roll(value, 8, 1, stride=8, stride_axis=0)
+        flipped.append(classes[kind].T)
+        for z in range(4):
+            classes[kind, pl.ds(edge_row(z + 1) + 1, 16), :] = planes[kind, z]
     flat = planes.reshape(128, 128)
     sides = [flat[pl.ds(0, 8, stride=16), :], flat[pl.ds(15, 8, stride=16), :]]
-    for kind in range(2):
-        for z in range(4):
-            classes[kind, pl.ds(edge_row(z + 1) + 1, 16), :] = planes[kind, z]
-    flipped = [classes[kind].T for kind in range(2)]
     tail = jnp.zeros((6, 128), F32)
     for side, y in ((0, 0), (1, 127)):
         ends[side, 1] = jnp.concatenate([flipped[0][y : y + 1], flipped[1][y : y + 1], tail], 0)
+
+    loads[10].wait()
+    count = jnp.int32(0)
+    order = []
+    for b in range(BLOCKS):
+        across = tile_ref[b] & 31
+        touches = jnp.where((across == 0) | (across == 31), 1, 0)
+        order.append((touches, count))
+        count = count + touches
+    listed[0] = count
+    for k in range(BLOCKS):
+        at = jnp.int32(0)
+        for b in range(k, BLOCKS):
+            touches, before = order[b]
+            at = at + jnp.where(before == k, b * touches, 0)
+        listed[k + 1] = at
 
     for dz in (-1, 1):
         pair = Z_PAIR[dz]
@@ -491,7 +525,15 @@
 
         where_z(dz, add)
 
-    loads[10].wait()
+    columns = []
+    for kind in range(2):
+        flipped = classes[kind].T
+        for y in (0, 127):
+            value = jnp.zeros((1, 128), F32)
+            for x in range(16):
+                at = (y + 8 * x) & 127
+                value = jnp.where((place[:1] & 15) == x, flipped[at : at + 1], value)
+            columns.append(value)
     bvel = [bvel_ref[i] for i in range(3)]
     rows = speed.reshape(3 * XN * 8, 128)
     for z in range(6):
@@ -515,26 +557,30 @@
         lanes, row, cell, frac, alive, down, across = particle(
             b, tile_ref, live_ref, cells_ref, offsets_ref
         )
-        left_high, left_low = split(speed[:, pl.ds(4 * down, 6)].reshape(144, 128))
-        right_high, right_low = wy[b, pl.ds(0, 128)], wy[b, pl.ds(128, 128)]
-        found = dot(
-            jnp.concatenate([left_high, left_low], 1),
-            jnp.concatenate([right_high, right_high], 0),
-            NN,
-        ) + dot(left_high, right_low, NN)
-        plain = found[:, :128].reshape(3, 6, 8, 128)
-        moment = found[:, 128:].reshape(3, 6, 8, 128)
+        start = place_of(down, across)
+        group = lax.shift_right_logical((lane - start) & 127, 3)
+        back = (128 - start) & 127
+        high, low = [], []
+        for pair in range(3):
+            value = speed[pair, pl.ds(4 * down, 6)]
+            part = value[5]
+            for i in range(5):
+                part = jnp.where(group == i, value[i], part)
+            part = jnp.where(lane < 48, pltpu.roll(part, back, 1), 0.0)
+            rounded = part.astype(BF16).astype(F32)
+            high.append(rounded + pltpu.roll(rounded, 64, 1))
+            low.append(part - rounded)
+        found = dot(jnp.concatenate(high + low, 0).astype(BF16), weights[b], NN)
+        found = found[:24] + found[24:]
         wz, wz_moment = along_z(cell, frac[0])
-        wx, wx_moment = six(near_x(cell), *spline(frac[1]))
         totals = [zero] * 4
         for pair in range(3):
-            sum_w = sum(wx[i] * plain[pair, i] for i in range(6))
-            sum_x = sum(wx_moment[i] * plain[pair, i] for i in range(6))
-            sum_y = sum(wx[i] * moment[pair, i] for i in range(6))
-            totals[0] = totals[0] + wz[pair] * sum_w
-            totals[1] = totals[1] + wz_moment[pair] * sum_w
-            totals[2] = totals[2] + wz[pair] * sum_x
-            totals[3] = totals[3] + wz[pair] * sum_y
+            rows_of = slice(8 * pair, 8 * pair + 8)
+            plain = found[rows_of, :128]
+            totals[0] = totals[0] + wz[pair] * plain
+            totals[1] = totals[1] + wz_moment[pair] * plain
+            totals[2] = totals[2] + wz[pair] * found[rows_of, 128:256]
+            totals[3] = totals[3] + wz[pair] * found[rows_of, 256:]
         totals = [(t + pltpu.roll(t, 7, 0)) * alive for t in totals]
         for i in range(3):
             here = 2 * i + 2
@@ -551,7 +597,6 @@
 
     lax.fori_loop(0, BLOCKS // UNROLL, gather_some, 0)
 
-    flipped = [classes[kind].T for kind in range(2)]
     inner = lane < 120
     totals = [ends[0, 0], ends[1, 0]]
     marks = [zero, zero]
@@ -591,8 +636,8 @@
         jnp.concatenate(
             [
                 marks[0][kind : kind + 1],
-                flipped[kind][0:1],
-                flipped[kind][127:128],
+                columns[2 * kind],
+                columns[2 * kind + 1],
                 marks[1][kind : kind + 1],
             ],
             0,
@@ -634,6 +679,7 @@
     affine_ref,
     moved_ref,
     edge_speed,
+    listed,
     out_velocity,
     out_affine,
     out_offsets,
@@ -642,47 +688,43 @@
     out_affine[...] = affine_ref[...]
     out_offsets[...] = moved_ref[...]
 
-    def one(b, carry):
-        across = tile_ref[b] & 31
-
-        @pl.when((across == 0) | (across == 31))
-        def _():
-            lanes, row, cell, frac, alive, down, across = particle(
-                b, tile_ref, live_ref, cells_ref, offsets_ref
-            )
-            side = jnp.where(across == 0, 0, 1)
-            value = edge_speed[side]
-            left = jnp.concatenate(
-                [pltpu.roll(value, (128 - edge_row(z) - 4 * down) & 127, 1) for z in range(6)], 0
-            )
-            left_high, left_low = split(left)
-            right = jnp.concatenate(
-                [along_x_rows(cell, frac[1]), jnp.zeros((120, 256), F32)], 0
-            )
-            right_high, right_low = split(right)
-            found = dot(left_high, right_high, NN) + (
-                dot(left_low, right_high, NN) + dot(left_high, right_low, NN)
-            )
-            we, we_moment = along_edge(cell, frac[2], across)
-            wz, wz_moment = six(near_z(cell), *spline(frac[0]))
-            sum_w = sum(wz[z] * found[8 * z : 8 * z + 8, :128] for z in range(6))
-            sum_z = sum(wz_moment[z] * found[8 * z : 8 * z + 8, :128] for z in range(6))
-            sum_x = sum(wz[z] * found[8 * z : 8 * z + 8, 128:] for z in range(6))
-            totals = [we * sum_w, we * sum_z, we * sum_x, we_moment * sum_w]
-            totals = [(t + pltpu.roll(t, 7, 0)) * alive for t in totals]
-            for i in range(3):
-                here = 2 * i + 2
-                moved = totals[0][here : here + 1]
-                out_velocity[pl.ds(i, 1), lanes] += moved
-                out_offsets[pl.ds(i, 1), lanes] += DT * moved
-                for j in range(3):
-                    out_affine[pl.ds(3 * i + j, 1), lanes] += (
-                        4.0 * totals[j + 1][here : here + 1]
-                    )
-
+    def one(k, carry):
+        b = listed[k + 1]
+        lanes, row, cell, frac, alive, down, across = particle(
+            b, tile_ref, live_ref, cells_ref, offsets_ref
+        )
+        side = jnp.where(across == 0, 0, 1)
+        value = edge_speed[side]
+        left = jnp.concatenate(
+            [pltpu.roll(value, (128 - edge_row(z) - 4 * down) & 127, 1) for z in range(6)], 0
+        )
+        left_high, left_low = split(left)
+        right = jnp.concatenate(
+            [along_x_rows(cell, frac[1]), jnp.zeros((120, 256), F32)], 0
+        )
+        right_high, right_low = split(right)
+        found = dot(left_high, right_high, NN) + (
+            dot(left_low, right_high, NN) + dot(left_high, right_low, NN)
+        )
+        we, we_moment = along_edge(cell, frac[2], across)
+        wz, wz_moment = six(near_z(cell), *spline(frac[0]))
+        sum_w = sum(wz[z] * found[8 * z : 8 * z + 8, :128] for z in range(6))
+        sum_z = sum(wz_moment[z] * found[8 * z : 8 * z + 8, :128] for z in range(6))
+        sum_x = sum(wz[z] * found[8 * z : 8 * z + 8, 128:] for z in range(6))
+        totals = [we * sum_w, we * sum_z, we * sum_x, we_moment * sum_w]
+        totals = [(t + pltpu.roll(t, 7, 0)) * alive for t in totals]
+        for i in range(3):
+            here = 2 * i + 2
+            moved = totals[0][here : here + 1]
+            out_velocity[pl.ds(i, 1), lanes] += moved
+            out_offsets[pl.ds(i, 1), lanes] += DT * moved
+            for j in range(3):
+                out_affine[pl.ds(3 * i + j, 1), lanes] += (
+                    4.0 * totals[j + 1][here : here + 1]
+                )
         return carry
 
-    lax.fori_loop(0, BLOCKS, one, 0)
+    lax.fori_loop(0, listed[0], one, 0)
 
 
 def on_device(
@@ -726,13 +768,14 @@
             pltpu.VMEM((9, count), F32),
             pltpu.VMEM((3, count), F32),
             pltpu.VMEM((2, 8, 128), F32),
+            pltpu.SMEM((BLOCKS + 1,), jnp.int32),
         ),
         in_specs=[hbm] * len(args),
-        out_specs=(smem,) * 2 + (vmem,) * 6,
+        out_specs=(smem,) * 2 + (vmem,) * 6 + (smem,),
         scratch_shapes=[pltpu.SMEM((3,), F32)]
         + [pltpu.VMEM(arg.shape, arg.dtype) for arg in args[5:]]
         + [
-            pltpu.VMEM((BLOCKS, 256, 256), BF16),
+            pltpu.VMEM((BLOCKS, 128, 384), BF16),
             pltpu.VMEM((STEP * BLOCKS + 12, 3, 8, 128), F32),
             pltpu.VMEM((3, TILES, 8, 128), F32),
             pltpu.VMEM((2, 9, 8, 128), F32),
@@ -760,7 +803,7 @@
             jax.ShapeDtypeStruct((9, count), F32),
             jax.ShapeDtypeStruct((3, count), F32),
         ),
-        in_specs=[smem] * 2 + [vmem] * 6,
+        in_specs=[smem] * 2 + [vmem] * 6 + [smem],
         out_specs=(vmem,) * 3,
         compiler_params=pltpu.CompilerParams(vmem_limit_bytes=VMEM_FINISH),
     )(*kept)

time: 22.1 us -> 21.5 us (0.973)
  Pallas kernels: 20.7 us -> 20.1 us
    pallas_call x1, Pallas kernels: 19.5 us -> 19.2 us  [on_device(): pl.pallas_call(spread, out_shape=(pltpu.SMEM((BLOCKS,), jnp.int32), pltpu...]
    pallas_call x1, Pallas kernels: 1.16 us -> 0.93 us  [on_device(): pl.pallas_call(finish, out_shape=(jax.ShapeDtypeStruct((3, count), F32),...]
where the time goes in v5:
time: 21.5 us; the launch traced here: 21.4 us
  Pallas kernels  20.1 us (93%)
  between operations  1.29 us (6%)
    pallas_call x1, Pallas kernels, on_device(): pl.pallas_call(spread, out_shape=(pltpu.SMEM((BLOCKS,), jnp.int32), pltpu...  19.2 us
    pallas_call x1, Pallas kernels, on_device(): pl.pallas_call(finish, out_shape=(jax.ShapeDtypeStruct((3, count), F32),...  0.93 us

profile of v5, /device:TPU:1, one launch (start us, length us, event | category | flops | bytes accessed | tf_op | source)
XLA Modules:
  0.0 21.4 jit_solution(15192217782049852200)
XLA Ops:
  1.3 19.2 %shard_map.130 = (s32[16]{0:T(128)S(4)}, s32[1]{0:T(128)S(4)}, s32[16,128]{1,0:T(8,128)S(1)}, f32[3,2048]{1,0:T(4,128)S(1)}, f32[3,2048]{1,0:T(4,128)S(1)}, /*in...) custom-call(s32[16]{0:T(128)} %tile_hbm.1, s32[1]{0:T(128)S(6)} %copy.14.live_hbm, ...), custom_call_target="tpu_custom_call" | custom-call | tf_op jit(solution)/shard_map/pallas_call | solution.py:760
  20.5 0.9 %shard_map.131 = (f32[3,2048]{1,0:T(4,128)}, f32[9,2048]{1,0:T(8,128)}, f32[3,2048]{1,0:T(4,128)}) custom-call(s32[16]{0:T(128)S(4)} %get-tuple-element.12.tile_ref, s32[1]{0:T(128)S(4)} %get-tuple-element.13.live_ref, s32[16,128]{1,0:T(8,128)S(1)} %get-tuple-element.14.cells_ref, f32[3,2048]{1,0:T(4,128)S(1)} %get-tuple-element.15.offsets_ref, ...), custom_call_target="tpu_custom_call" | custom-call | tf_op jit(solution)/shard_map/pallas_call | solution.py:799

commit v6 on v5

--- a/solution.py
+++ b/solution.py
@@ -249,12 +249,13 @@
     nx, ny, nz = lax.axis_size("gx"), lax.axis_size("gy"), lax.axis_size("gz")
     above, below = iz < nz - 1, iz > 0
 
+    def beside_of(i, n):
+        return {-1: jnp.where(i == 0, n - 1, i - 1), 0: i, 1: jnp.where(i == n - 1, 0, i + 1)}
+
+    at_x, at_y, at_z = beside_of(ix, nx), beside_of(iy, ny), beside_of(iz, nz)
+
     def device(dz, dx, dy):
-        return {
-            "gx": lax.rem(ix + dx + nx, nx),
-            "gy": lax.rem(iy + dy + ny, ny),
-            "gz": lax.rem(iz + dz + nz, nz),
-        }
+        return {"gx": at_x[dx], "gy": at_y[dy], "gz": at_z[dz]}
 
     def where_z(dz, action):
         if dz == 0:
@@ -487,43 +488,52 @@
             where_z(dz, start)
 
     pl.when(iy == ny - 1)(lambda: send_ends(1))
-    for dz, dx in FACES:
-        where_z(dz, grid_sends[-dz, -dx].start)
+    for dz in (1, -1, 0):
+
+        def start(dz=dz):
+            for dx in (1, -1, 0):
+                if (dz, dx) != (0, 0):
+                    grid_sends[-dz, -dx].start()
+
+        where_z(dz, start)
     pl.when(iy != ny - 1)(lambda: send_ends(1))
     send_ends(-1)
 
-    for dz, dx in FACES:
-
-        def add(dz=dz, dx=dx):
-            grid_sends[dz, dx].wait_recv()
-            if dx == 0:
-                pair = Z_PAIR[dz]
-                came = got_z.at[(1 - dz) // 2]
-                speed[pair] = speed[pair] + came[pl.ds(FIRST, XN)]
-                z = 0 if dz == -1 else 5
-                for kind in range(2):
-                    classes[kind, pl.ds(edge_row(z) + 1, 16), :] = came[
-                        pl.ds(PLANE + 2 * kind, 2)
-                    ].reshape(16, 128)
-                return
-            x = 0 if dx == -1 else 17
-            xs = pl.ds(8 + 8 * dx, 2)
-            first, mark = (0, 3) if dx == -1 else (2, 0)
-            if dz == 0:
-                came = got_x.at[(1 - dx) // 2]
-                speed[:, xs] = speed[:, xs] + came[pl.ds(0, 6)].reshape(3, 2, 8, 128)
-                tile, depths = came[8], range(4)
-            else:
-                pair = Z_PAIR[dz]
-                came = got_zx.at[1 - dz + (1 - dx) // 2]
-                speed[pair, xs] = speed[pair, xs] + came[pl.ds(first, 2)]
-                tile, depths = came[mark], (Z_PLANE[-dz],)
-            for kind in range(2):
-                for z in depths:
-                    at = edge_row(z + 1 + 4 * dz) + x
-                    classes[kind, pl.ds(at, 1), :] = tile[4 * kind + z : 4 * kind + z + 1]
-
-        where_z(dz, add)
+    for dz in (0, 1, -1):
+
+        def wait(dz=dz):
+            for dx in (-1, 0, 1):
+                if (dz, dx) != (0, 0):
+                    grid_sends[dz, dx].wait_recv()
+
+        where_z(dz, wait)
+    there = {-1: below, 1: above}
+    for dx in (-1, 1):
+        came = got_x.at[(1 - dx) // 2]
+        xs = pl.ds(8 + 8 * dx, 2)
+        speed[:, xs] = speed[:, xs] + came[pl.ds(0, 6)].reshape(3, 2, 8, 128)
+    for dz in (-1, 1):
+        pair = Z_PAIR[dz]
+        came = got_z[(1 - dz) // 2, pl.ds(FIRST, XN)]
+        parts = [got_zx[1 - dz + (1 - dx) // 2, pl.ds(0 if dx == -1 else 2, 2)] for dx in (-1, 1)]
+        came = jnp.concatenate(
+            [came[:2] + parts[0], came[2:16], came[16:] + parts[1]], 0
+        )
+        speed[pair] = speed[pair] + jnp.where(there[dz], came, 0.0)
+    for kind in range(2):
+        for dx, x, mark in ((-1, 0, 3), (1, 17, 0)):
+            for z in range(4):
+                classes[kind, pl.ds(edge_row(z + 1) + x, 1), :] = got_x[
+                    (1 - dx) // 2, 8, pl.ds(4 * kind + z, 1), :
+                ]
+            for dz in (-1, 1):
+                classes[kind, pl.ds(edge_row(0 if dz == -1 else 5) + x, 1), :] = got_zx[
+                    1 - dz + (1 - dx) // 2, mark, pl.ds(4 * kind + Z_PLANE[-dz], 1), :
+                ]
+        for dz in (-1, 1):
+            classes[kind, pl.ds(edge_row(0 if dz == -1 else 5) + 1, 16), :] = got_z[
+                (1 - dz) // 2, pl.ds(PLANE + 2 * kind, 2)
+            ].reshape(16, 128)
 
     columns = []
     for kind in range(2):
@@ -598,6 +608,14 @@
     lax.fori_loop(0, BLOCKS // UNROLL, gather_some, 0)
 
     inner = lane < 120
+    for dz in (0, 1, -1):
+
+        def wait(dz=dz):
+            for dx in (-1, 0, 1):
+                for dy in (-1, 1):
+                    end_sends[dz, dx, dy].wait_recv()
+
+        where_z(dz, wait)
     totals = [ends[0, 0], ends[1, 0]]
     marks = [zero, zero]
     for dz, dx in NINE:
@@ -627,7 +645,6 @@
             for side in range(2):
                 totals[side] = totals[side] + moved(got_x[(1 - dx) // 2, 6 + side])
         for dy in (-1, 1):
-            where_z(dz, end_sends[dz, dx, dy].wait_recv)
             side = (1 + dy) // 2
             came = got_ends.at[1 - side, SLOT[-dz, -dx]]
             totals[side] = totals[side] + moved(came[0])

time: 21.5 us -> 21.1 us (0.981)
  Pallas kernels: 20.1 us -> 19.7 us
    pallas_call x1, Pallas kernels: 19.2 us -> 18 us  [on_device(): pl.pallas_call(spread, out_shape=(pltpu.SMEM((BLOCKS,), jnp.int32), pltpu...]
    pallas_call x1, Pallas kernels: 0.93 us -> 1.65 us  [on_device(): pl.pallas_call(finish, out_shape=(jax.ShapeDtypeStruct((3, count), F32),...]
where the time goes in v6:
time: 21.1 us; the launch traced here: 21 us
  Pallas kernels  19.7 us (93%)
  between operations  1.29 us (6%)
    pallas_call x1, Pallas kernels, on_device(): pl.pallas_call(spread, out_shape=(pltpu.SMEM((BLOCKS,), jnp.int32), pltpu...  18 us
    pallas_call x1, Pallas kernels, on_device(): pl.pallas_call(finish, out_shape=(jax.ShapeDtypeStruct((3, count), F32),...  1.65 us

profile of v6, /device:TPU:1, one launch (start us, length us, event | category | flops | bytes accessed | tf_op | source)
XLA Modules:
  0.0 21.0 jit_solution(13055478404666543269)
XLA Ops:
  1.3 18.0 %shard_map.130 = (s32[16]{0:T(128)S(4)}, s32[1]{0:T(128)S(4)}, s32[16,128]{1,0:T(8,128)S(1)}, f32[3,2048]{1,0:T(4,128)S(1)}, f32[3,2048]{1,0:T(4,128)S(1)}, /*in...) custom-call(s32[16]{0:T(128)} %tile_hbm.1, s32[1]{0:T(128)S(6)} %copy.14.live_hbm, ...), custom_call_target="tpu_custom_call" | custom-call | tf_op jit(solution)/shard_map/pallas_call | solution.py:777
  19.3 1.7 %shard_map.131 = (f32[3,2048]{1,0:T(4,128)}, f32[9,2048]{1,0:T(8,128)}, f32[3,2048]{1,0:T(4,128)}) custom-call(s32[16]{0:T(128)S(4)} %get-tuple-element.12.tile_ref, s32[1]{0:T(128)S(4)} %get-tuple-element.13.live_ref, s32[16,128]{1,0:T(8,128)S(1)} %get-tuple-element.14.cells_ref, f32[3,2048]{1,0:T(4,128)S(1)} %get-tuple-element.15.offsets_ref, ...), custom_call_target="tpu_custom_call" | custom-call | tf_op jit(solution)/shard_map/pallas_call | solution.py:816

commit v7 on v6

--- a/solution.py
+++ b/solution.py
@@ -12,7 +12,6 @@
 FRICTION = (0.1, 0.4, 0.8, 1.2)
 
 BLOCKS = 16
-UNROLL = 16
 VMEM_SPREAD = 58 * 1024 * 1024
 VMEM_FINISH = 16 * 1024 * 1024
 XN = 18
@@ -145,7 +144,7 @@
 
 
 def particle(b, tile_ref, live_ref, cells_ref, offsets_ref):
-    lanes = pl.ds(pl.multiple_of(b * 128, 128), 128)
+    lanes = pl.ds(b * 128 if isinstance(b, int) else pl.multiple_of(b * 128, 128), 128)
 
     def row(ref, r):
         return jnp.broadcast_to(ref[pl.ds(r, 1), lanes], (8, 128))
@@ -324,11 +323,23 @@
         return carry
 
     lax.fori_loop(0, BLOCKS, clear, 0)
-    for load in loads[:8]:
+    for load in loads:
         load.wait()
 
     zero = jnp.zeros((8, 128), F32)
     lane = lax.broadcasted_iota(jnp.int32, (8, 128), 1)
+
+    flipped = []
+    for kind, source in enumerate((mask_ref, friction_ref)):
+        for z in range(4):
+            value = source[z].astype(F32)
+            classes[kind, pl.ds(edge_row(z + 1) + 1, 16), :] = value
+            planes[kind, z] = pltpu.roll(value, 8, 1, stride=8, stride_axis=0)
+        flipped.append(classes[kind].T)
+        for z in range(4):
+            classes[kind, pl.ds(edge_row(z + 1) + 1, 16), :] = planes[kind, z]
+    flat = planes.reshape(128, 128)
+    sides = [flat[pl.ds(0, 8, stride=16), :], flat[pl.ds(15, 8, stride=16), :]]
 
     def scatter(b, edges):
         lanes, row, cell, frac, alive, down, across = particle(
@@ -389,12 +400,9 @@
             out.append(edges[2 * z + 1] + high * part)
         return tuple(out)
 
-    def scatter_some(step, edges):
-        for u in range(UNROLL):
-            edges = scatter(step * UNROLL + u, edges)
-        return edges
-
-    edges = lax.fori_loop(0, BLOCKS // UNROLL, scatter_some, (zero,) * 12)
+    edges = (zero,) * 12
+    for b in range(BLOCKS):
+        edges = scatter(b, edges)
 
     half = jnp.where(lane >= 60, lane - 60, lane)
     pair_of = jnp.where(half >= 2 * STEP, 2, jnp.where(half >= STEP, 1, 0))
@@ -410,24 +418,64 @@
             total = total + part
         ends[side, 0] = total
 
-    loads[8].wait()
-    loads[9].wait()
-    flipped = []
-    for kind, source in enumerate((mask_ref, friction_ref)):
-        for z in range(4):
-            value = source[z].astype(F32)
-            classes[kind, pl.ds(edge_row(z + 1) + 1, 16), :] = value
-            planes[kind, z] = pltpu.roll(value, 8, 1, stride=8, stride_axis=0)
-        flipped.append(classes[kind].T)
-        for z in range(4):
-            classes[kind, pl.ds(edge_row(z + 1) + 1, 16), :] = planes[kind, z]
-    flat = planes.reshape(128, 128)
-    sides = [flat[pl.ds(0, 8, stride=16), :], flat[pl.ds(15, 8, stride=16), :]]
     tail = jnp.zeros((6, 128), F32)
     for side, y in ((0, 0), (1, 127)):
         ends[side, 1] = jnp.concatenate([flipped[0][y : y + 1], flipped[1][y : y + 1], tail], 0)
 
-    loads[10].wait()
+    for dz in (-1, 1):
+        pair = Z_PAIR[dz]
+        grid[pair, pl.ds(PLANE, 4)] = planes[:, Z_PLANE[dz]].reshape(4, 8, 128)
+        grid[pair, LEFT] = sides[0]
+        grid[pair, RIGHT] = sides[1]
+        here = pair_of == pair
+        shift = (-STEP * dz) % 128
+
+        def beside(first, second):
+            moved = pltpu.roll(jnp.where(here, second, 0.0), shift, 1)
+            return jnp.where(here, first, 0.0) + moved
+
+        both = beside(ends[0, 0], ends[1, 0])
+        grid[pair, EDGE_A] = both
+        grid[pair, EDGE_B] = both
+        for side in range(2):
+            ends_z[(1 + dz) // 2, side] = beside(ends[side, 0], ends[side, 1])
+    for side in range(2):
+        across_x[side, 6] = ends[0, 0]
+        across_x[side, 7] = ends[1, 0]
+        across_x[side, 8] = sides[side]
+
+    for pair in range(3):
+        total = jnp.zeros((XN, 8, 128), F32)
+        for b in range(BLOCKS):
+            down = lax.shift_right_logical(tile_ref[b], 5) & 3
+            total = total + patch[pl.ds(STEP * b + 12 - 4 * down, XN), pair]
+        grid[pair, pl.ds(FIRST, XN)] = total
+        speed[pair] = total
+        across_x[0, pl.ds(2 * pair, 2)] = total[:2]
+        across_x[1, pl.ds(2 * pair, 2)] = total[16:]
+
+    pl.semaphore_wait(
+        barrier, 26 - 9 * (1 - above.astype(jnp.int32)) - 9 * (1 - below.astype(jnp.int32))
+    )
+    def send_ends(dy):
+        for dz in (1, -1, 0):
+
+            def start(dz=dz):
+                for dx in (1, -1, 0):
+                    end_sends[-dz, -dx, -dy].start()
+
+            where_z(dz, start)
+
+    send_ends(1)
+    send_ends(-1)
+    for dz in (1, -1, 0):
+
+        def start(dz=dz):
+            for dx in (1, -1, 0):
+                if (dz, dx) != (0, 0):
+                    grid_sends[-dz, -dx].start()
+
+        where_z(dz, start)
     count = jnp.int32(0)
     order = []
     for b in range(BLOCKS):
@@ -442,62 +490,6 @@
             touches, before = order[b]
             at = at + jnp.where(before == k, b * touches, 0)
         listed[k + 1] = at
-
-    for dz in (-1, 1):
-        pair = Z_PAIR[dz]
-        grid[pair, pl.ds(PLANE, 4)] = planes[:, Z_PLANE[dz]].reshape(4, 8, 128)
-        grid[pair, LEFT] = sides[0]
-        grid[pair, RIGHT] = sides[1]
-        here = pair_of == pair
-        shift = (-STEP * dz) % 128
-
-        def beside(first, second):
-            moved = pltpu.roll(jnp.where(here, second, 0.0), shift, 1)
-            return jnp.where(here, first, 0.0) + moved
-
-        both = beside(ends[0, 0], ends[1, 0])
-        grid[pair, EDGE_A] = both
-        grid[pair, EDGE_B] = both
-        for side in range(2):
-            ends_z[(1 + dz) // 2, side] = beside(ends[side, 0], ends[side, 1])
-    for side in range(2):
-        across_x[side, 6] = ends[0, 0]
-        across_x[side, 7] = ends[1, 0]
-        across_x[side, 8] = sides[side]
-
-    for pair in range(3):
-        total = jnp.zeros((XN, 8, 128), F32)
-        for b in range(BLOCKS):
-            down = lax.shift_right_logical(tile_ref[b], 5) & 3
-            total = total + patch[pl.ds(STEP * b + 12 - 4 * down, XN), pair]
-        grid[pair, pl.ds(FIRST, XN)] = total
-        speed[pair] = total
-        across_x[0, pl.ds(2 * pair, 2)] = total[:2]
-        across_x[1, pl.ds(2 * pair, 2)] = total[16:]
-
-    pl.semaphore_wait(
-        barrier, 26 - 9 * (1 - above.astype(jnp.int32)) - 9 * (1 - below.astype(jnp.int32))
-    )
-    def send_ends(dy):
-        for dz in (1, -1, 0):
-
-            def start(dz=dz):
-                for dx in (1, -1, 0):
-                    end_sends[-dz, -dx, -dy].start()
-
-            where_z(dz, start)
-
-    pl.when(iy == ny - 1)(lambda: send_ends(1))
-    for dz in (1, -1, 0):
-
-        def start(dz=dz):
-            for dx in (1, -1, 0):
-                if (dz, dx) != (0, 0):
-                    grid_sends[-dz, -dx].start()
-
-        where_z(dz, start)
-    pl.when(iy != ny - 1)(lambda: send_ends(1))
-    send_ends(-1)
 
     for dz in (0, 1, -1):
 
@@ -600,12 +592,8 @@
             for j in range(3):
                 out_affine[pl.ds(3 * i + j, 1), lanes] = 4.0 * totals[j + 1][here : here + 1]
 
-    def gather_some(step, carry):
-        for u in range(UNROLL):
-            gather(step * UNROLL + u)
-        return carry
-
-    lax.fori_loop(0, BLOCKS // UNROLL, gather_some, 0)
+    for b in range(BLOCKS):
+        gather(b)
 
     inner = lane < 120
     for dz in (0, 1, -1):
@@ -705,7 +693,7 @@
     out_affine[...] = affine_ref[...]
     out_offsets[...] = moved_ref[...]
 
-    def one(k, carry):
+    def share(k):
         b = listed[k + 1]
         lanes, row, cell, frac, alive, down, across = particle(
             b, tile_ref, live_ref, cells_ref, offsets_ref
@@ -729,19 +717,23 @@
         sum_z = sum(wz_moment[z] * found[8 * z : 8 * z + 8, :128] for z in range(6))
         sum_x = sum(wz[z] * found[8 * z : 8 * z + 8, 128:] for z in range(6))
         totals = [we * sum_w, we * sum_z, we * sum_x, we_moment * sum_w]
-        totals = [(t + pltpu.roll(t, 7, 0)) * alive for t in totals]
-        for i in range(3):
-            here = 2 * i + 2
-            moved = totals[0][here : here + 1]
-            out_velocity[pl.ds(i, 1), lanes] += moved
-            out_offsets[pl.ds(i, 1), lanes] += DT * moved
-            for j in range(3):
-                out_affine[pl.ds(3 * i + j, 1), lanes] += (
-                    4.0 * totals[j + 1][here : here + 1]
-                )
+        used = jnp.where(k < listed[0], alive, 0.0)
+        return lanes, [(t + pltpu.roll(t, 7, 0)) * used for t in totals]
+
+    def two(step, carry):
+        for lanes, totals in [share(2 * step + u) for u in range(2)]:
+            for i in range(3):
+                here = 2 * i + 2
+                moved = totals[0][here : here + 1]
+                out_velocity[pl.ds(i, 1), lanes] += moved
+                out_offsets[pl.ds(i, 1), lanes] += DT * moved
+                for j in range(3):
+                    out_affine[pl.ds(3 * i + j, 1), lanes] += (
+                        4.0 * totals[j + 1][here : here + 1]
+                    )
         return carry
 
-    lax.fori_loop(0, listed[0], one, 0)
+    lax.fori_loop(0, lax.shift_right_logical(listed[0] + 1, 1), two, 0)
 
 
 def on_device(

time: 21.1 us -> 20.6 us (0.976)
  Pallas kernels: 19.7 us -> 19.3 us
    pallas_call x1, Pallas kernels: 1.65 us -> 1.23 us  [on_device(): pl.pallas_call(finish, out_shape=(jax.ShapeDtypeStruct((3, count), F32),...]
where the time goes in v7:
time: 20.6 us
  Pallas kernels  19.3 us (94%)
  between operations  1.29 us (6%)
    pallas_call x1, Pallas kernels, on_device(): pl.pallas_call(spread, out_shape=(pltpu.SMEM((BLOCKS,), jnp.int32), pltpu...  18.1 us
    pallas_call x1, Pallas kernels, on_device(): pl.pallas_call(finish, out_shape=(jax.ShapeDtypeStruct((3, count), F32),...  1.23 us

profile of v7, /device:TPU:1, one launch (start us, length us, event | category | flops | bytes accessed | tf_op | source)
XLA Modules:
  0.0 20.6 jit_solution(15360395520472453173)
XLA Ops:
  1.3 18.1 %shard_map.130 = (s32[16]{0:T(128)S(4)}, s32[1]{0:T(128)S(4)}, s32[16,128]{1,0:T(8,128)S(1)}, f32[3,2048]{1,0:T(4,128)S(1)}, f32[3,2048]{1,0:T(4,128)S(1)}, /*in...) custom-call(s32[16]{0:T(128)} %tile_hbm.1, s32[1]{0:T(128)S(6)} %copy.14.live_hbm, ...), custom_call_target="tpu_custom_call" | custom-call | tf_op jit(solution)/shard_map/pallas_call | solution.py:769
  19.3 1.2 %shard_map.131 = (f32[3,2048]{1,0:T(4,128)}, f32[9,2048]{1,0:T(8,128)}, f32[3,2048]{1,0:T(4,128)}) custom-call(s32[16]{0:T(128)S(4)} %get-tuple-element.12.tile_ref, s32[1]{0:T(128)S(4)} %get-tuple-element.13.live_ref, s32[16,128]{1,0:T(8,128)S(1)} %get-tuple-element.14.cells_ref, f32[3,2048]{1,0:T(4,128)S(1)} %get-tuple-element.15.offsets_ref, ...), custom_call_target="tpu_custom_call" | custom-call | tf_op jit(solution)/shard_map/pallas_call | solution.py:808

commit v8 on v7

--- a/solution.py
+++ b/solution.py
@@ -314,7 +314,7 @@
                 dst = got_ends.at[side, SLOT[dz, dx], 0]
             end_sends[-dz, -dx, -dy] = sender(src, dst, dz, dx, dy)
 
-    speed[...] = jnp.zeros((3, XN, 8, 128), F32)
+    speed[...] = jnp.zeros((4, XN, 8, 128), F32)
     classes[...] = jnp.zeros((2, 128, 128), F32)
     patch[pl.ds(0, 12)] = jnp.zeros((12, 3, 8, 128), F32)
 
@@ -503,7 +503,7 @@
     for dx in (-1, 1):
         came = got_x.at[(1 - dx) // 2]
         xs = pl.ds(8 + 8 * dx, 2)
-        speed[:, xs] = speed[:, xs] + came[pl.ds(0, 6)].reshape(3, 2, 8, 128)
+        speed[pl.ds(0, 3), xs] = speed[pl.ds(0, 3), xs] + came[pl.ds(0, 6)].reshape(3, 2, 8, 128)
     for dz in (-1, 1):
         pair = Z_PAIR[dz]
         came = got_z[(1 - dz) // 2, pl.ds(FIRST, XN)]
@@ -537,7 +537,7 @@
                 value = jnp.where((place[:1] & 15) == x, flipped[at : at + 1], value)
             columns.append(value)
     bvel = [bvel_ref[i] for i in range(3)]
-    rows = speed.reshape(3 * XN * 8, 128)
+    rows = speed.reshape(4 * XN * 8, 128)
     for z in range(6):
         pair, low = z // 2, z % 2
 
@@ -788,7 +788,7 @@
             pltpu.VMEM((STEP * BLOCKS + 12, 3, 8, 128), F32),
             pltpu.VMEM((3, TILES, 8, 128), F32),
             pltpu.VMEM((2, 9, 8, 128), F32),
-            pltpu.VMEM((3, XN, 8, 128), F32),
+            pltpu.VMEM((4, XN, 8, 128), F32),
             pltpu.VMEM((2, 2, 8, 128), F32),
             pltpu.VMEM((2, 2, 8, 128), F32),
             pltpu.VMEM((2, 128, 128), F32),

time: 20.6 us -> 20.6 us (level); the launches traced: 20.6 us -> 20.3 us
  Pallas kernels: 19.3 us -> 19 us
    pallas_call x1, Pallas kernels: 1.23 us -> 0.96 us  [on_device(): pl.pallas_call(finish, out_shape=(jax.ShapeDtypeStruct((3, count), F32),...]
where the time goes in v8:
time: 20.6 us; the launch traced here: 20.3 us
  Pallas kernels  19 us (92%)
  between operations  1.29 us (6%)
    pallas_call x1, Pallas kernels, on_device(): pl.pallas_call(spread, out_shape=(pltpu.SMEM((BLOCKS,), jnp.int32), pltpu...  18.1 us
    pallas_call x1, Pallas kernels, on_device(): pl.pallas_call(finish, out_shape=(jax.ShapeDtypeStruct((3, count), F32),...  0.96 us

profile of v8, /device:TPU:1, one launch (start us, length us, event | category | flops | bytes accessed | tf_op | source)
XLA Modules:
  0.0 20.3 jit_solution(13983080206171814151)
XLA Ops:
  1.3 18.1 %shard_map.130 = (s32[16]{0:T(128)S(4)}, s32[1]{0:T(128)S(4)}, s32[16,128]{1,0:T(8,128)S(1)}, f32[3,2048]{1,0:T(4,128)S(1)}, f32[3,2048]{1,0:T(4,128)S(1)}, /*in...) custom-call(s32[16]{0:T(128)} %tile_hbm.1, s32[1]{0:T(128)S(6)} %copy.14.live_hbm, ...), custom_call_target="tpu_custom_call" | custom-call | tf_op jit(solution)/shard_map/pallas_call | solution.py:769
  19.3 1.0 %shard_map.131 = (f32[3,2048]{1,0:T(4,128)}, f32[9,2048]{1,0:T(8,128)}, f32[3,2048]{1,0:T(4,128)}) custom-call(s32[16]{0:T(128)S(4)} %get-tuple-element.12.tile_ref, s32[1]{0:T(128)S(4)} %get-tuple-element.13.live_ref, s32[16,128]{1,0:T(8,128)S(1)} %get-tuple-element.14.cells_ref, f32[3,2048]{1,0:T(4,128)S(1)} %get-tuple-element.15.offsets_ref, ...), custom_call_target="tpu_custom_call" | custom-call | tf_op jit(solution)/shard_map/pallas_call | solution.py:808
